TPU v7x, 256 devices: a whole 4x4x8 slice. The times are simulated.
256 devices in a mesh: row: 16 (over x, z_lo, core), col: 16 (over y, z_hi).
Axes of the slice: x: 4, y: 4, z: 8 (z_hi: 4, z_lo: 2; z = z_hi * 2 + z_lo), core: 2. Of those that a mesh axis runs over, the one named last changes fastest.
Arguments:
- sequence_features: bfloat16 [1280, 64, 128], P(('row', 'col')), may hold values from -6 to 6
- first_projection: bfloat16 [64, 32], replicated, may hold values from -0.75 to 0.75
- second_projection: bfloat16 [64, 32], replicated, may hold values from -0.75 to 0.75
- final_projection: bfloat16 [1024, 128], replicated, may hold values from -0.1875 to 0.1875
- final_offset: float32 [128], replicated, may hold values from -3 to 3
- edge_change_cotangent: bfloat16 [1280, 1280, 128], P('row', 'col'), may hold values from -6 to 6
Outputs:
- pair_delta: bfloat16 [1280, 1280, 128], P('row', 'col')
- alignment_gradient: float32 [1280, 64, 128], P(('row', 'col'))
- left_weight_gradient: float32 [64, 32], replicated
- right_weight_gradient: float32 [64, 32], replicated
- output_weight_gradient: float32 [1024, 128], replicated
- bias_gradient: float32 [128], replicated
All inputs are finite; a program needn't handle non-finite values.
Results may differ from a plain program's by a relative error of at most 0.022.
Values may be sent and summed in bfloat16 or wider, within the bound.
No kernel may reach another device: no remote copies, remote signals or barrier semaphores. Data moves between devices by JAX's collectives and lax.ppermute only.
A program may use at most 64 MiB of HBM per device.

v0:
```python
import functools

import jax
import jax.numpy as jnp
from jax import lax
from jax.experimental import pallas as pl
from jax.experimental.pallas import tpu as pltpu
from jax.sharding import PartitionSpec as P

BF = jnp.bfloat16
F32 = jnp.float32
LANES = 128
VMEM = 56 * 1024 * 1024


def exchange(x, axis):
    return lax.all_to_all(x, axis, 0, 0, tiled=True)


def gather_blocks(x, axis):
    return exchange(jnp.broadcast_to(x[None], (lax.axis_size(axis), *x.shape)), axis)


def scatter_blocks(x, axis):
    n = lax.axis_size(axis)
    x = exchange(x.reshape(n, x.shape[0] // n, *x.shape[1:]), axis)
    return jnp.sum(x.astype(F32), axis=0)


def swap_axes(x):
    n = lax.axis_size("row")
    return lax.ppermute(
        x, ("row", "col"), [(r * n + c, c * n + r) for r in range(n) for c in range(n)]
    )


def project_kernel(scale, x_ref, w_ref, out_ref):
    for n in range(x_ref.shape[0]):
        block = lax.dot_general(
            w_ref[...], x_ref[n], (((0,), (0,)), ((), ())), preferred_element_type=F32
        ).astype(BF)
        block = (block.astype(F32) * scale).astype(BF)
        for copy in range(out_ref.shape[0]):
            out_ref[copy, n] = block


def project_copies(source, weight, scale, copies):
    owned, _, sequences = source.shape
    return pl.pallas_call(
        functools.partial(project_kernel, scale),
        out_shape=jax.ShapeDtypeStruct((copies, owned, weight.shape[1], sequences), BF),
        compiler_params=pltpu.CompilerParams(vmem_limit_bytes=16 << 20),
        cost_estimate=pl.CostEstimate(flops=1 << 22, bytes_accessed=1 << 20, transcendentals=0),
        name="project_copies",
    )(source, weight)


def padded_rows(t, rows):
    return jnp.concatenate([t, jnp.zeros((rows - t.shape[0], t.shape[1]), t.dtype)], axis=0)


def outer_grad_kernel(width, group, t_ref, w_ref, g_ref, bias_ref):
    @pl.when(pl.program_id(0) == 0)
    def _():
        bias_ref[...] = jnp.zeros_like(bias_ref)

    channels = w_ref.shape[0]
    total = jnp.zeros((1, LANES), F32)
    for pair in range(group // 2):
        a, b = t_ref[2 * pair], t_ref[2 * pair + 1]
        total = total + jnp.sum(a.astype(F32) + b.astype(F32), axis=0, keepdims=True)
        both = jnp.concatenate([padded_rows(a, LANES), padded_rows(b, LANES)], axis=0)
        grad = lax.dot_general(
            w_ref[...], both, (((1,), (1,)), ((), ())), preferred_element_type=F32
        ).astype(BF)
        for half in range(2):
            row = (2 * pair + half) * width
            for d in range(channels // width):
                g_ref[pl.ds(row, width), pl.ds(d * LANES, LANES)] = grad[
                    d * width : (d + 1) * width, half * LANES : (half + 1) * LANES
                ]
    bias_ref[...] += jnp.broadcast_to(total, bias_ref.shape)


def stream(hbm_ref, buf_ref, sem_ref, pieces):
    rows = buf_ref.shape[0] // pieces
    out = []
    for k in range(pieces):
        part = pl.ds(k * rows, rows)
        copy = pltpu.make_async_copy(hbm_ref.at[part], buf_ref.at[part], sem_ref.at[k])
        copy.start()
        out.append((part, copy))
    return out


def left_grad_kernel(scale, pieces, r_ref, g_ref, out_ref, buf_ref, pad_ref, sem_ref):
    copies = stream(g_ref, buf_ref, sem_ref, pieces)
    columns, sequences = r_ref.shape[1:]
    for d in range(r_ref.shape[0]):
        pad_ref[pl.ds(d * LANES, LANES)] = padded_rows(r_ref[d], LANES)
    for part, copy in copies:
        copy.wait()
        out_ref[part] = (
            jnp.dot(buf_ref[part], pad_ref[...], preferred_element_type=F32) * scale
        ).astype(out_ref.dtype)


def right_grad_kernel(pieces, l_ref, g_ref, out_ref, buf_ref, acc_ref, sem_ref):
    copies = stream(g_ref, buf_ref, sem_ref, pieces)
    chunk = 512
    for k, (part, copy) in enumerate(copies):
        lt = l_ref[part].T
        copy.wait()
        for n in range(acc_ref.shape[1] // chunk):
            lanes = pl.ds(n * chunk, chunk)
            term = jnp.dot(lt, buf_ref[part, lanes], preferred_element_type=F32)
            acc_ref[:, lanes] = term if k == 0 else acc_ref[:, lanes] + term
    columns = out_ref.shape[1]
    for d in range(out_ref.shape[0]):
        block = acc_ref[:, d * LANES : (d + 1) * LANES].T
        out_ref[d] = block[:columns].astype(out_ref.dtype)


def pair_kernel(
    width, group, l_ref, r_ref, t_ref, wt_ref, off_ref, p_ref, gw_ref, rt_ref, outer_ref
):
    columns = t_ref.shape[1]
    depth = r_ref.shape[0]

    @pl.when(pl.program_id(0) == 0)
    def _():
        gw_ref[...] = jnp.zeros_like(gw_ref)
        for d in range(depth):
            rt_ref[:, pl.ds(d * LANES, LANES)] = padded_rows(r_ref[d], LANES).T

    per = 4
    for n in range(depth // per):
        block = jnp.dot(
            l_ref[...], rt_ref[:, pl.ds(n * per * LANES, per * LANES)], preferred_element_type=F32
        ).astype(BF)
        for i in range(group):
            for d in range(per):
                outer_ref[pl.ds((n * per + d) * width, width), pl.ds(i * LANES, LANES)] = block[
                    i * width : (i + 1) * width, d * LANES : (d + 1) * LANES
                ]
    offset = off_ref[...]
    out = jnp.dot(wt_ref[...], outer_ref[...], preferred_element_type=F32)
    for i in range(group):
        p_ref[i] = (out[:, i * LANES : (i + 1) * LANES].T[:columns] + offset).astype(BF)
    cotangent = jnp.concatenate([padded_rows(t_ref[i], LANES) for i in range(group)], axis=0)
    step = 256
    for n in range(gw_ref.shape[0] // step):
        part = pl.ds(n * step, step)
        gw_ref[part] += jnp.dot(outer_ref[part], cotangent, preferred_element_type=F32)


def params():
    return pltpu.CompilerParams(
        dimension_semantics=("arbitrary",), vmem_limit_bytes=VMEM
    )


def outer_grads(cotangent, weight, width):
    rows, columns, out = cotangent.shape
    group = 16
    channels = weight.shape[0]
    depth = channels // width
    return pl.pallas_call(
        functools.partial(outer_grad_kernel, width, group),
        grid=(rows // group,),
        in_specs=[
            pl.BlockSpec((group, columns, out), lambda i: (i, 0, 0)),
            pl.BlockSpec((channels, out), lambda i: (0, 0)),
        ],
        out_specs=[
            pl.BlockSpec((group * width, depth * LANES), lambda i: (i, 0)),
            pl.BlockSpec((8, out), lambda i: (0, 0)),
        ],
        out_shape=[
            jax.ShapeDtypeStruct((rows * width, depth * LANES), BF),
            jax.ShapeDtypeStruct((8, out), F32),
        ],
        compiler_params=params(),
        cost_estimate=pl.CostEstimate(
            flops=4 * rows * columns * channels * out, bytes_accessed=22 << 20, transcendentals=0
        ),
        name="outer_grads",
    )(cotangent, weight)


def left_grads(right, grad, scale):
    rows, depth = grad.shape
    sequences = right.shape[2]
    pieces = 10
    return pl.pallas_call(
        functools.partial(left_grad_kernel, scale, pieces),
        in_specs=[
            pl.BlockSpec(memory_space=pltpu.VMEM),
            pl.BlockSpec(memory_space=pl.ANY),
        ],
        out_specs=pl.BlockSpec(memory_space=pltpu.VMEM),
        out_shape=jax.ShapeDtypeStruct((rows, sequences), BF),
        scratch_shapes=[
            pltpu.VMEM((rows, depth), BF),
            pltpu.VMEM((depth, sequences), BF),
            pltpu.SemaphoreType.DMA((pieces,)),
        ],
        compiler_params=pltpu.CompilerParams(vmem_limit_bytes=VMEM),
        cost_estimate=pl.CostEstimate(
            flops=4 * rows * depth * sequences, bytes_accessed=22 << 20, transcendentals=0
        ),
        name="left_grads",
    )(right, grad)


def right_grads(left, grad, columns):
    rows, sequences = left.shape
    depth = grad.shape[1]
    pieces = 10
    return pl.pallas_call(
        functools.partial(right_grad_kernel, pieces),
        in_specs=[
            pl.BlockSpec(memory_space=pltpu.VMEM),
            pl.BlockSpec(memory_space=pl.ANY),
        ],
        out_specs=pl.BlockSpec(memory_space=pltpu.VMEM),
        out_shape=jax.ShapeDtypeStruct((depth // LANES, columns, sequences), BF),
        scratch_shapes=[
            pltpu.VMEM((rows, depth), BF),
            pltpu.VMEM((sequences, depth), F32),
            pltpu.SemaphoreType.DMA((pieces,)),
        ],
        compiler_params=pltpu.CompilerParams(vmem_limit_bytes=VMEM),
        cost_estimate=pl.CostEstimate(
            flops=4 * rows * depth * sequences, bytes_accessed=22 << 20, transcendentals=0
        ),
        name="right_grads",
    )(left, grad)


def pairs(left, right, cotangent, weight_t, offset, width):
    rows, columns, out = cotangent.shape
    sequences = left.shape[1]
    channels = weight_t.shape[1]
    group = 20
    depth = right.shape[0]
    return pl.pallas_call(
        functools.partial(pair_kernel, width, group),
        grid=(rows // group,),
        in_specs=[
            pl.BlockSpec((group * width, sequences), lambda i: (i, 0)),
            pl.BlockSpec(right.shape, lambda i: (0, 0, 0)),
            pl.BlockSpec((group, columns, out), lambda i: (i, 0, 0)),
            pl.BlockSpec((out, channels), lambda i: (0, 0)),
            pl.BlockSpec((1, out), lambda i: (0, 0)),
        ],
        out_specs=[
            pl.BlockSpec((group, columns, out), lambda i: (i, 0, 0)),
            pl.BlockSpec((channels, out), lambda i: (0, 0)),
        ],
        out_shape=[
            jax.ShapeDtypeStruct((rows, columns, out), BF),
            jax.ShapeDtypeStruct((channels, out), F32),
        ],
        scratch_shapes=[
            pltpu.VMEM((sequences, depth * LANES), BF),
            pltpu.VMEM((channels, group * LANES), BF),
        ],
        compiler_params=params(),
        cost_estimate=pl.CostEstimate(
            flops=12 * rows * LANES * channels * out, bytes_accessed=6 << 20, transcendentals=0
        ),
        name="pairs",
    )(left, right, cotangent, weight_t, offset)


def after(value, *others):
    return lax.optimization_barrier((value, *others))[0]


def shards(
    sequence_features,
    first_projection,
    second_projection,
    final_projection,
    final_offset,
    edge_change_cotangent,
):
    n_row = lax.axis_size("row")
    n_col = lax.axis_size("col")
    owned, _, sequences = sequence_features.shape
    rows, columns, out = edge_change_cotangent.shape
    width = first_projection.shape[1]
    scale = 1.0 / sequences

    weight = final_projection.reshape(width, width, out).swapaxes(0, 1).reshape(-1, out)
    weight_t = weight.T
    channels = weight.shape[0]
    offset = final_offset.reshape(1, out)

    swapped = swap_axes(sequence_features)
    left = project_copies(sequence_features, first_projection, scale, n_col)
    grad, bias_local = outer_grads(edge_change_cotangent, after(weight, left), width)
    left = exchange(left, "col").reshape(rows * width, sequences)

    right = project_copies(
        swapped, after(second_projection, bias_local, weight_t), 1.0, n_row
    )
    right = exchange(right, "row").reshape(columns, width, sequences).swapaxes(0, 1)

    right_part = right_grads(left, grad, columns)
    left_part = left_grads(after(right, right_part), grad, scale)
    right_sum = scatter_blocks(right_part.swapaxes(0, 1), "row")

    pair_delta, weight_part = pairs(
        left, right, edge_change_cotangent, weight_t, after(offset, left_part, right_sum), width
    )
    left_sum = scatter_blocks(left_part.reshape(rows, width, sequences), "col")

    exact = lax.Precision.HIGHEST
    left_weight = jnp.einsum(
        "gph,gah->ap", sequence_features.astype(F32), left_sum, precision=exact
    )
    right_weight = jnp.einsum("gph,gah->ap", swapped.astype(F32), right_sum, precision=exact)
    right_sum = swap_axes(right_sum)
    alignment_gradient = jnp.einsum(
        "awr,iw->air", left_sum, first_projection.astype(F32), precision=exact
    ) + jnp.einsum("awr,iw->air", right_sum, second_projection.astype(F32), precision=exact)

    small = jnp.concatenate(
        [left_weight.reshape(-1, LANES), right_weight.reshape(-1, LANES), bias_local]
    )
    extra = small.shape[0]
    each = -(-extra // n_row)
    small = jnp.pad(small, ((0, each * n_row - extra), (0, 0))).reshape(n_row, each, LANES)
    main = channels // n_row
    pack = -(-(main + each) // 8) * 8
    total = jnp.concatenate([weight_part.reshape(n_row, main, out), small], axis=1)
    total = jnp.pad(total, ((0, 0), (0, pack - main - each), (0, 0))).astype(BF)
    total = scatter_blocks(total.reshape(n_row * pack, out), "row").astype(BF)
    total = jnp.sum(gather_blocks(total, "col").astype(F32), axis=0).astype(BF)
    total = gather_blocks(total, "row")
    total = total.astype(F32) * (1.0 / (owned * n_row * n_col))
    small = total[:, main : main + each].reshape(-1, LANES)
    total = total[:, :main].reshape(width, width, out).swapaxes(0, 1).reshape(channels, out)
    size = left_weight.size // LANES
    return (
        pair_delta,
        alignment_gradient,
        small[:size].reshape(left_weight.shape).T,
        small[size : 2 * size].reshape(right_weight.shape).T,
        total,
        small[2 * size],
    )


def solution(mesh):
    placed = (P(("row", "col"), None, None), P(), P(), P(), P(), P("row", "col", None))
    return jax.shard_map(
        shards,
        mesh=mesh,
        in_specs=placed,
        out_specs=(P("row", "col", None), P(("row", "col"), None, None), P(), P(), P(), P()),
        check_vma=False,
    )
```

profile of v0, /device:TPU:38, one launch (start us, length us, event | category | flops | bytes accessed | tf_op | source)
XLA Modules:
  0.0 158.4 jit_solution(4182290227607977430)
XLA Ops:
  0.6 0.8 copy.29.w_ref
  1.4 0.0 copy-start
  1.4 0.9 copy-done
  2.3 0.0 copy-start.1
  2.3 0.0 copy-start.4
  2.3 1.1 project_copies.2
  3.4 10.3 %all-to-all-start = ((bf16[16,5,32,128]{3,2,1,0:T(8,128)(2,1)}), bf16[16,5,32,128]{3,2,1,0:T(8,128)(2,1)S(1)}, u32[]{:S(2)}, u32[]{:S(2)}) async-start(bf16[16,5,32,128]{3,2,1,0:T(8,128)(2,1)} %project_copies.2), calls=%async_computation | async-start | bytes 1310720 | tf_op jit(solution)/shard_map/all_to_all | solution.py:17
  13.7 0.0 copy-done.1
  13.7 9.3 %collective-permute-start = (bf16[5,64,128]{2,1,0:T(8,128)(2,1)S(1)}, bf16[5,64,128]{2,1,0:T(8,128)(2,1)S(1)}, u32[]{:S(2)}, u32[]{:S(2)}) collective-permute-start(bf16[5,64,128]{2,1,0:T(8,128)(2,1)S(1)} %copy-done.1), channel_id=1, source_target_pairs={{0,0},{1,16},{2,32},{3,48},{4,64},{5,80},{6,96},{7,112},{8,128},{9... | collective-permute-start | bytes 245768 | tf_op jit(solution)/shard_map/ppermute | solution.py:32
  23.0 0.0 copy-done.4
  23.0 0.8 copy.30
  23.8 0.0 copy-start.3
  23.8 0.0 copy-start.6
  23.8 11.6 %outer_grads.1 = (bf16[2560,4096]{1,0:T(8,128)(2,1)}, f32[8,128]{1,0:T(8,128)}) custom-call(bf16[80,80,128]{2,1,0:T(8,128)(2,1)} %t_ref.3, bf16[1024,128]{1,0:T(8,128)(2,1)} %bitcast.54), custom_call_target="tpu_custom_call" | custom-call | flops 3355443200 | bytes 23068672 | tf_op jit(solution)/shard_map/outer_grads/pallas_call | solution.py:168
  35.4 0.0 copy-done.3
  35.4 0.9 copy.31
  36.3 0.0 copy-done.6
  36.3 0.1 copy.32.w_ref
  36.4 1.8 %collective-permute-done.x_ref = bf16[5,64,128]{2,1,0:T(8,128)(2,1)S(1)} collective-permute-done((bf16[5,64,128]{2,1,0:T(8,128)(2,1)S(1)}, bf16[5,64,128]{2,1,0:T(8,128)(2,1)S(1)}, u32[]{:S(2)}, u32[]{:S(2)}) %collective-permute-start) | collective-permute-done | bytes 81952 | tf_op jit(solution)/shard_map/ppermute | solution.py:32
  38.2 1.1 project_copies.3
  39.3 0.0 all-to-all-done
  39.3 0.0 copy-start.2
  39.3 6.5 %all-to-all-start.1 = ((bf16[16,5,32,128]{3,2,1,0:T(8,128)(2,1)}), bf16[16,5,32,128]{3,2,1,0:T(8,128)(2,1)S(1)}, u32[]{:S(2)}, u32[]{:S(2)}) async-start(bf16[16,5,32,128]{3,2,1,0:T(8,128)(2,1)} %project_copies.3), calls=%async_computation.1 | async-start | bytes 1310720 | tf_op jit(solution)/shard_map/all_to_all | solution.py:17
  45.8 0.0 copy-done.2
  45.8 9.6 %right_grads.1 = bf16[32,80,128]{2,1,0:T(8,128)(2,1)} custom-call(bf16[2560,128]{1,0:T(8,128)(2,1)} %bitcast.45, bf16[2560,4096]{1,0:T(8,128)(2,1)} %get-tuple-element.17.g_ref), custom_call_target="tpu_custom_call" | custom-call | flops 5368709120 | bytes 23068672 | tf_op jit(solution)/shard_map/right_grads/pallas_call | solution.py:220
  55.4 0.0 copy-start.7
  55.4 2.1 %copy.34 = bf16[80,32,128]{2,1,0:T(8,128)(2,1)} copy(bf16[80,32,128]{2,0,1:T(8,128)(2,1)} %bitcast.50) | data formatting | bytes 1310720 | tf_op jit(solution)/shard_map/transpose | solution.py:313
  57.5 0.0 all-to-all-done.1
  57.5 5.7 %all-to-all-start.2 = ((bf16[16,5,32,128]{3,2,1,0:T(8,128)(2,1)}), bf16[16,5,32,128]{3,2,1,0:T(8,128)(2,1)S(1)}, u32[]{:S(2)}, u32[]{:S(2)}) async-start(bf16[16,5,32,128]{3,2,1,0:T(8,128)(2,1)} %bitcast.9), calls=%async_computation.2 | async-start | bytes 1310720 | tf_op jit(solution)/shard_map/all_to_all | solution.py:17
  63.2 0.0 copy-done.7
  63.2 1.1 copy.37
  64.3 10.6 %left_grads.1 = bf16[2560,128]{1,0:T(8,128)(2,1)} custom-call(bf16[32,80,128]{2,1,0:T(8,128)(2,1)} %bitcast.48, bf16[2560,4096]{1,0:T(8,128)(2,1)} %get-tuple-element.17.g_ref), custom_call_target="tpu_custom_call" | custom-call | flops 5368709120 | bytes 23068672 | tf_op jit(solution)/shard_map/left_grads/pallas_call | solution.py:195
  74.9 0.0 all-to-all-done.2
  75.0 3.6 %all-to-all-start.3 = ((bf16[16,5,32,128]{3,2,1,0:T(8,128)(2,1)}), bf16[16,5,32,128]{3,2,1,0:T(8,128)(2,1)S(1)}, u32[]{:S(2)}, u32[]{:S(2)}) async-start(bf16[16,5,32,128]{3,2,1,0:T(8,128)(2,1)} %bitcast.47), calls=%async_computation.3 | async-start | bytes 1310720 | tf_op jit(solution)/shard_map/all_to_all | solution.py:17
  78.6 0.1 convert_reduce_fusion.1
  78.7 0.2 fusion.2
  78.9 0.1 reshape.71
  79.0 17.0 %pairs.1 = (bf16[80,80,128]{2,1,0:T(8,128)(2,1)}, f32[1024,128]{1,0:T(8,128)}) custom-call(bf16[2560,128]{1,0:T(8,128)(2,1)} %bitcast.46, bf16[32,80,128]{2,1,0:T(8,128)(2,1)} %bitcast.49, bf16[80,80,128]{2,1,0:T(8,128)(2,1)} %t_ref.3, bf16[128,1024]{1,0:T(8,128)(2,1)} %bitcast.58, f32[1,128]{1,0:T(1,128)} %bitcast.61), custom_call_target="tpu_custom_call" | custom-call | flops 16106127360 | bytes 6291456 | tf_op jit(solution)/shard_map/pairs/pallas_call | solution.py:247
  96.0 1.1 convert.23
  97.0 3.5 %all-to-all-done.3 = bf16[16,5,32,128]{3,2,1,0:T(8,128)(2,1)S(1)} async-done(((bf16[16,5,32,128]{3,2,1,0:T(8,128)(2,1)}), bf16[16,5,32,128]{3,2,1,0:T(8,128)(2,1)S(1)}, u32[]{:S(2)}, u32[]{:S(2)}) %all-to-all-start.3) | async-done | bytes 655392 | tf_op jit(solution)/shard_map/all_to_all | solution.py:17
  100.6 0.1 convert_reduce_fusion
  100.7 0.2 fusion.1
  100.9 0.1 reshape.70
  101.0 0.0 copy-start.5
  101.0 10.5 %all_to_all.35 = bf16[16,72,128]{2,1,0:T(8,128)(2,1)S(1)} all-to-all(bf16[16,72,128]{2,1,0:T(8,128)(2,1)S(1)} %fusion.5), channel_id=1, replica_groups=mesh['row'=16,'col'=16] {'row'}, dimensions={0} | all-to-all | bytes 589824 | tf_op jit(solution)/shard_map/all_to_all | solution.py:17
  111.6 19.9 %all_to_all.36 = bf16[16,72,128]{2,1,0:T(8,128)(2,1)S(1)} all-to-all(bf16[16,72,128]{2,1,0:T(8,128)(2,1)S(1)} %broadcast_in_dim.4), channel_id=1, replica_groups=mesh['row'=16,'col'=16] {'col'}, dimensions={0} | all-to-all | bytes 589824 | tf_op jit(solution)/shard_map/all_to_all | solution.py:17
  131.6 0.8 broadcast_in_dim.5
  132.4 6.8 %all-to-all-start.6 = ((bf16[16,72,128]{2,1,0:T(8,128)(2,1)}), bf16[16,72,128]{2,1,0:T(8,128)(2,1)S(1)}, u32[]{:S(2)}, u32[]{:S(2)}) async-start(bf16[16,72,128]{2,1,0:T(8,128)(2,1)} %broadcast_in_dim.5), calls=%async_computation.6 | async-start | bytes 589824 | tf_op jit(solution)/shard_map/all_to_all | solution.py:17
  139.1 1.9 %collective-permute-start.1 = (f32[5,32,128]{2,1,0:T(8,128)S(1)}, f32[5,32,128]{2,1,0:T(8,128)S(1)}, u32[]{:S(2)}, u32[]{:S(2)}) collective-permute-start(f32[5,32,128]{2,1,0:T(8,128)S(1)} %convert_reduce_fusion.1), channel_id=1, source_target_pairs={{0,0},{1,16},{2,32},{3,48},{4,64},{5,80},{6,96},{7,112},{8,128},{9... | collective-permute-start | bytes 245768 | tf_op jit(solution)/shard_map/ppermute | solution.py:32
  141.0 0.0 copy-done.5
  141.1 0.3 fusion.12
  141.3 13.0 %collective-permute-done.1 = f32[5,32,128]{2,1,0:T(8,128)S(1)} collective-permute-done((f32[5,32,128]{2,1,0:T(8,128)S(1)}, f32[5,32,128]{2,1,0:T(8,128)S(1)}, u32[]{:S(2)}, u32[]{:S(2)}) %collective-permute-start.1) | collective-permute-done | bytes 81952 | tf_op jit(solution)/shard_map/ppermute | solution.py:32
  154.4 0.9 fusion
  155.3 0.0 all-to-all-done.6
  155.5 0.5 slice_bitcast_fusion
  156.0 1.1 copy.35
  157.1 0.7 reshape.75
  157.8 0.7 reshape.74
  (12 shorter events, 0.3 us)
Async XLA Ops:
  1.4 0.9 copy-start
  2.3 11.4 %copy-start.1 = (bf16[5,64,128]{2,1,0:T(8,128)(2,1)S(1)}, bf16[5,64,128]{2,1,0:T(8,128)(2,1)}, u32[]{:S(2)}) copy-start(bf16[5,64,128]{2,1,0:T(8,128)(2,1)} %x_ref.1) | copy-start | bytes 245764
  2.3 20.7 %copy-start.4 = (bf16[1024,128]{1,0:T(8,128)(2,1)S(1)}, bf16[1024,128]{1,0:T(8,128)(2,1)}, u32[]{:S(2)}) copy-start(bf16[1024,128]{1,0:T(8,128)(2,1)} %param.9) | copy-start | bytes 786436
  3.4 35.9 %all-to-all-start = ((bf16[16,5,32,128]{3,2,1,0:T(8,128)(2,1)}), bf16[16,5,32,128]{3,2,1,0:T(8,128)(2,1)S(1)}, u32[]{:S(2)}, u32[]{:S(2)}) async-start(bf16[16,5,32,128]{3,2,1,0:T(8,128)(2,1)} %project_copies.2), calls=%async_computation | async-start | bytes 1310720 | tf_op jit(solution)/shard_map/all_to_all | solution.py:17
  13.7 24.5 %collective-permute-start = (bf16[5,64,128]{2,1,0:T(8,128)(2,1)S(1)}, bf16[5,64,128]{2,1,0:T(8,128)(2,1)S(1)}, u32[]{:S(2)}, u32[]{:S(2)}) collective-permute-start(bf16[5,64,128]{2,1,0:T(8,128)(2,1)S(1)} %copy-done.1), channel_id=1, source_target_pairs={{0,0},{1,16},{2,32},{3,48},{4,64},{5,80},{6,96},{7,112},{8,128},{9... | collective-permute-start | bytes 245768 | tf_op jit(solution)/shard_map/ppermute | solution.py:32
  23.8 11.6 %copy-start.3 = (bf16[32,32,128]{2,1,0:T(8,128)(2,1)S(1)}, bf16[32,32,128]{2,1,0:T(8,128)(2,1)}, u32[]{:S(2)}) copy-start(bf16[32,32,128]{2,1,0:T(8,128)(2,1)} %copy.30) | copy-start | bytes 786436
  23.8 12.4 %copy-start.6 = (bf16[64,32]{0,1:T(8,128)(2,1)S(1)}, bf16[64,32]{0,1:T(8,128)(2,1)}, u32[]{:S(2)}) copy-start(bf16[64,32]{0,1:T(8,128)(2,1)} %param.8) | copy-start | bytes 12292
  39.3 6.5 %copy-start.2 = (bf16[16,5,32,128]{3,2,1,0:T(8,128)(2,1)}, bf16[16,5,32,128]{3,2,1,0:T(8,128)(2,1)S(1)}, u32[]{:S(2)}) copy-start(bf16[16,5,32,128]{3,2,1,0:T(8,128)(2,1)S(1)} %all-to-all-done) | copy-start | bytes 1966084
  39.3 18.2 %all-to-all-start.1 = ((bf16[16,5,32,128]{3,2,1,0:T(8,128)(2,1)}), bf16[16,5,32,128]{3,2,1,0:T(8,128)(2,1)S(1)}, u32[]{:S(2)}, u32[]{:S(2)}) async-start(bf16[16,5,32,128]{3,2,1,0:T(8,128)(2,1)} %project_copies.3), calls=%async_computation.1 | async-start | bytes 1310720 | tf_op jit(solution)/shard_map/all_to_all | solution.py:17
  55.4 7.9 %copy-start.7 = (f32[8,128]{1,0:T(8,128)S(1)}, f32[8,128]{1,0:T(8,128)}, u32[]{:S(2)}) copy-start(f32[8,128]{1,0:T(8,128)} %get-tuple-element.15) | copy-start | bytes 12292
  57.5 17.5 %all-to-all-start.2 = ((bf16[16,5,32,128]{3,2,1,0:T(8,128)(2,1)}), bf16[16,5,32,128]{3,2,1,0:T(8,128)(2,1)S(1)}, u32[]{:S(2)}, u32[]{:S(2)}) async-start(bf16[16,5,32,128]{3,2,1,0:T(8,128)(2,1)} %bitcast.9), calls=%async_computation.2 | async-start | bytes 1310720 | tf_op jit(solution)/shard_map/all_to_all | solution.py:17
  75.0 25.6 %all-to-all-start.3 = ((bf16[16,5,32,128]{3,2,1,0:T(8,128)(2,1)}), bf16[16,5,32,128]{3,2,1,0:T(8,128)(2,1)S(1)}, u32[]{:S(2)}, u32[]{:S(2)}) async-start(bf16[16,5,32,128]{3,2,1,0:T(8,128)(2,1)} %bitcast.47), calls=%async_computation.3 | async-start | bytes 1310720 | tf_op jit(solution)/shard_map/all_to_all | solution.py:17
  101.0 40.0 %copy-start.5 = (bf16[64,32]{0,1:T(8,128)(2,1)S(1)}, bf16[64,32]{0,1:T(8,128)(2,1)}, u32[]{:S(2)}) copy-start(bf16[64,32]{0,1:T(8,128)(2,1)} %param.7) | copy-start | bytes 12292
  132.4 22.9 %all-to-all-start.6 = ((bf16[16,72,128]{2,1,0:T(8,128)(2,1)}), bf16[16,72,128]{2,1,0:T(8,128)(2,1)S(1)}, u32[]{:S(2)}, u32[]{:S(2)}) async-start(bf16[16,72,128]{2,1,0:T(8,128)(2,1)} %broadcast_in_dim.5), calls=%async_computation.6 | async-start | bytes 589824 | tf_op jit(solution)/shard_map/all_to_all | solution.py:17
  139.1 15.2 %collective-permute-start.1 = (f32[5,32,128]{2,1,0:T(8,128)S(1)}, f32[5,32,128]{2,1,0:T(8,128)S(1)}, u32[]{:S(2)}, u32[]{:S(2)}) collective-permute-start(f32[5,32,128]{2,1,0:T(8,128)S(1)} %convert_reduce_fusion.1), channel_id=1, source_target_pairs={{0,0},{1,16},{2,32},{3,48},{4,64},{5,80},{6,96},{7,112},{8,128},{9... | collective-permute-start | bytes 245768 | tf_op jit(solution)/shard_map/ppermute | solution.py:32
where the time goes:
time: 159 us; the launch traced here: 158 us
  Pallas kernels  50.9 us (32%)
  starting transfers between devices  44.1 us (28%)
  blocking collectives  30.4 us (19%)
  waiting for transfers between devices  18.4 us (12%)
  local copies, waits for them, and re-layouts  10.7 us (7%)
  matrix products  1.62 us (1%)
    all_to_all x5, starting transfers between devices, exchange(): return lax.all_to_all(x, axis, 0, 0, tiled=True)  32.9 us
    all_to_all x2, blocking collectives, exchange(): return lax.all_to_all(x, axis, 0, 0, tiled=True)  30.4 us
    pallas_call x1, Pallas kernels, pairs(): pl.pallas_call(functools.partial(pair_kernel, width, group), grid=(rows /...  17 us
    ppermute x2, waiting for transfers between devices, swap_axes(): lax.ppermute(x, ('row', 'col'), [(r * n + c, c * n + r) for r in range(n)...  14.9 us
    pallas_call x1, Pallas kernels, outer_grads(): pl.pallas_call(functools.partial(outer_grad_kernel, width, group), grid=(...  11.6 us
    ppermute x2, starting transfers between devices, swap_axes(): lax.ppermute(x, ('row', 'col'), [(r * n + c, c * n + r) for r in range(n)...  11.2 us
    pallas_call x1, Pallas kernels, left_grads(): pl.pallas_call(functools.partial(left_grad_kernel, scale, pieces), in_spe...  10.6 us
    pallas_call x1, Pallas kernels, right_grads(): pl.pallas_call(functools.partial(right_grad_kernel, pieces), in_specs=[pl...  9.56 us
  transfers between devices with their start and end apart: 7, of which 3 were waited for; matrix products, arithmetic and copies ran while one was open for 5% of the time, Pallas kernels for 31%

commit v1 on v0

v1 whole, which is shorter than its diff:
```python
import functools

import jax
import jax.numpy as jnp
from jax import lax
from jax.experimental import pallas as pl
from jax.experimental.pallas import tpu as pltpu
from jax.sharding import PartitionSpec as P

BF = jnp.bfloat16
F32 = jnp.float32
LANES = 128
VMEM = 56 * 1024 * 1024


def exchange(x, axis):
    return lax.all_to_all(x, axis, 0, 0, tiled=True)


def gather_blocks(x, axis):
    return exchange(jnp.broadcast_to(x[None], (lax.axis_size(axis), *x.shape)), axis)


def scatter_blocks(x, axis):
    n = lax.axis_size(axis)
    x = exchange(x.reshape(n, x.shape[0] // n, *x.shape[1:]), axis)
    return jnp.sum(x.astype(F32), axis=0)


def swap_axes(x):
    n = lax.axis_size("row")
    return lax.ppermute(
        x, ("row", "col"), [(r * n + c, c * n + r) for r in range(n) for c in range(n)]
    )


def project_kernel(scale, x_ref, first_ref, second_ref, left_ref, right_ref):
    for n in range(x_ref.shape[0]):
        x = x_ref[n]
        left = jnp.dot(first_ref[...], x, preferred_element_type=F32).astype(BF)
        left = (left.astype(F32) * scale).astype(BF)
        for copy in range(left_ref.shape[0]):
            left_ref[copy, n] = left
        right_ref[n] = jnp.dot(second_ref[...], x, preferred_element_type=F32).astype(BF)


def project(source, first, second, scale, copies):
    owned, _, sequences = source.shape
    width = first.shape[0]
    return pl.pallas_call(
        functools.partial(project_kernel, scale),
        out_shape=[
            jax.ShapeDtypeStruct((copies, owned, width, sequences), BF),
            jax.ShapeDtypeStruct((owned, width, sequences), BF),
        ],
        compiler_params=pltpu.CompilerParams(vmem_limit_bytes=16 << 20),
        cost_estimate=pl.CostEstimate(flops=1 << 22, bytes_accessed=1 << 20, transcendentals=0),
        name="project",
    )(source, first, second)


def unpack_kernel(inverse, pack_ref, weight_ref, left_ref, right_ref, bias_ref):
    width = weight_ref.shape[0]
    blocks = pack_ref.shape[0]
    main = weight_ref.shape[0] * weight_ref.shape[1] // blocks
    each = width // blocks
    total = [pack_ref[n].astype(F32) * inverse for n in range(blocks)]
    weight = jnp.concatenate([t[:main] for t in total], axis=0).reshape(weight_ref.shape)
    weight_ref[...] = jnp.swapaxes(weight, 0, 1)
    half = left_ref.shape[1]
    for n in range(blocks):
        rows = total[n][main : main + each]
        left_ref[pl.ds(n * each, each)] = rows[:, :half]
        right_ref[pl.ds(n * each, each)] = rows[:, half:]
    bias_ref[...] = total[0][main + each : main + each + 1]


def unpack(packed, width, half, inverse):
    out = packed.shape[2]
    return pl.pallas_call(
        functools.partial(unpack_kernel, inverse),
        out_shape=[
            jax.ShapeDtypeStruct((width, width, out), F32),
            jax.ShapeDtypeStruct((width, half), F32),
            jax.ShapeDtypeStruct((width, half), F32),
            jax.ShapeDtypeStruct((1, out), F32),
        ],
        compiler_params=pltpu.CompilerParams(vmem_limit_bytes=16 << 20),
        cost_estimate=pl.CostEstimate(flops=1 << 20, bytes_accessed=1 << 20, transcendentals=0),
        name="unpack",
    )(packed)


def padded_rows(t, rows):
    return jnp.concatenate([t, jnp.zeros((rows - t.shape[0], t.shape[1]), t.dtype)], axis=0)


def outer_grad_kernel(width, pieces, t_ref, w_ref, g_ref, bias_ref, buf_ref, sem_ref):
    channels = w_ref.shape[0]
    group = t_ref.shape[0] // pieces
    total = jnp.zeros((1, LANES), F32)
    copies = []
    for k in range(pieces):
        for first in range(k * group, (k + 1) * group, 2):
            a, b = t_ref[first], t_ref[first + 1]
            total = total + jnp.sum(a.astype(F32) + b.astype(F32), axis=0, keepdims=True)
            both = jnp.concatenate([padded_rows(a, LANES), padded_rows(b, LANES)], axis=0)
            grad = lax.dot_general(
                w_ref[...], both, (((1,), (1,)), ((), ())), preferred_element_type=F32
            ).astype(BF)
            for half in range(2):
                row = (first + half) * width
                for d in range(channels // width):
                    buf_ref[pl.ds(row, width), pl.ds(d * LANES, LANES)] = grad[
                        d * width : (d + 1) * width, half * LANES : (half + 1) * LANES
                    ]
        part = pl.ds(k * group * width, group * width)
        copy = pltpu.make_async_copy(buf_ref.at[part], g_ref.at[part], sem_ref.at[k])
        copy.start()
        copies.append(copy)
    bias_ref[...] = jnp.broadcast_to(total, bias_ref.shape)
    for copy in copies:
        copy.wait()


def stream(hbm_ref, buf_ref, sem_ref, pieces):
    rows = buf_ref.shape[0] // pieces
    out = []
    for k in range(pieces):
        part = pl.ds(k * rows, rows)
        copy = pltpu.make_async_copy(hbm_ref.at[part], buf_ref.at[part], sem_ref.at[k])
        copy.start()
        out.append((part, copy))
    return out


def left_grad_kernel(scale, pieces, r_ref, g_ref, out_ref, panel_ref, buf_ref, pad_ref, sem_ref):
    copies = stream(g_ref, buf_ref, sem_ref, pieces)
    panel = jnp.swapaxes(r_ref[...].astype(F32), 0, 1).astype(BF)
    panel_ref[...] = panel
    for d in range(panel.shape[0]):
        pad_ref[pl.ds(d * LANES, LANES)] = padded_rows(panel[d], LANES)
    for part, copy in copies:
        copy.wait()
        out_ref[part] = (
            jnp.dot(buf_ref[part], pad_ref[...], preferred_element_type=F32) * scale
        ).astype(out_ref.dtype)


def right_grad_kernel(pieces, l_ref, g_ref, out_ref, buf_ref, acc_ref, block_ref, sem_ref):
    copies = stream(g_ref, buf_ref, sem_ref, pieces)
    chunk = 512
    for k, (part, copy) in enumerate(copies):
        lt = l_ref[part].T
        copy.wait()
        for n in range(acc_ref.shape[1] // chunk):
            lanes = pl.ds(n * chunk, chunk)
            term = jnp.dot(lt, buf_ref[part, lanes], preferred_element_type=F32)
            acc_ref[:, lanes] = term if k == 0 else acc_ref[:, lanes] + term
    columns, depth = out_ref.shape[:2]
    group = 8
    for first in range(0, depth, group):
        blocks = [
            acc_ref[:, d * LANES : (d + 1) * LANES].T[:columns]
            for d in range(first, first + group)
        ]
        block_ref[:, pl.ds(first, group)] = jnp.swapaxes(jnp.stack(blocks), 0, 1)
    out_ref[...] = block_ref[...].astype(out_ref.dtype)


def pair_kernel(
    width, group, l_ref, r_ref, t_ref, w_ref, off_ref, p_ref, pack_ref, gw_ref, wt_ref, rt_ref,
    outer_ref,
):
    columns = t_ref.shape[1]
    depth = r_ref.shape[0]

    @pl.when(pl.program_id(0) == 0)
    def _():
        gw_ref[...] = jnp.zeros_like(gw_ref)
        for n in range(w_ref.shape[0] // LANES):
            part = pl.ds(n * LANES, LANES)
            wt_ref[:, part] = w_ref[part].T
        for d in range(depth):
            rt_ref[:, pl.ds(d * LANES, LANES)] = padded_rows(r_ref[d], LANES).T

    per = 4
    for n in range(depth // per):
        block = jnp.dot(
            l_ref[...], rt_ref[:, pl.ds(n * per * LANES, per * LANES)], preferred_element_type=F32
        ).astype(BF)
        for i in range(group):
            for d in range(per):
                outer_ref[pl.ds((n * per + d) * width, width), pl.ds(i * LANES, LANES)] = block[
                    i * width : (i + 1) * width, d * LANES : (d + 1) * LANES
                ]
    offset = off_ref[...]
    out = jnp.dot(wt_ref[...], outer_ref[...], preferred_element_type=F32)
    for i in range(group):
        p_ref[i] = (out[:, i * LANES : (i + 1) * LANES].T[:columns] + offset).astype(BF)
    cotangent = jnp.concatenate([padded_rows(t_ref[i], LANES) for i in range(group)], axis=0)
    step = 256
    for n in range(gw_ref.shape[0] // step):
        part = pl.ds(n * step, step)
        gw_ref[part] += jnp.dot(outer_ref[part], cotangent, preferred_element_type=F32)

    @pl.when(pl.program_id(0) == pl.num_programs(0) - 1)
    def _():
        blocks, pack, out = pack_ref.shape
        main = gw_ref.shape[0] // blocks
        for n in range(blocks):
            block = padded_rows(gw_ref[pl.ds(n * main, main)], pack)
            pack_ref[n] = block.astype(BF)


def params():
    return pltpu.CompilerParams(
        dimension_semantics=("arbitrary",), vmem_limit_bytes=VMEM
    )


def outer_grads(cotangent, weight, width):
    rows, columns, out = cotangent.shape
    pieces = 10
    channels = weight.shape[0]
    depth = channels // width
    return pl.pallas_call(
        functools.partial(outer_grad_kernel, width, pieces),
        in_specs=[pl.BlockSpec(memory_space=pltpu.VMEM)] * 2,
        out_specs=[
            pl.BlockSpec(memory_space=pl.ANY),
            pl.BlockSpec(memory_space=pltpu.VMEM),
        ],
        out_shape=[
            jax.ShapeDtypeStruct((rows * width, depth * LANES), BF),
            jax.ShapeDtypeStruct((8, out), F32),
        ],
        scratch_shapes=[
            pltpu.VMEM((rows * width, depth * LANES), BF),
            pltpu.SemaphoreType.DMA((pieces,)),
        ],
        compiler_params=pltpu.CompilerParams(vmem_limit_bytes=VMEM),
        cost_estimate=pl.CostEstimate(
            flops=4 * rows * columns * channels * out, bytes_accessed=22 << 20, transcendentals=0
        ),
        name="outer_grads",
    )(cotangent, weight)


def left_grads(right, grad, scale):
    rows, depth = grad.shape
    sequences = right.shape[2]
    pieces = 10
    return pl.pallas_call(
        functools.partial(left_grad_kernel, scale, pieces),
        in_specs=[
            pl.BlockSpec(memory_space=pltpu.VMEM),
            pl.BlockSpec(memory_space=pl.ANY),
        ],
        out_specs=[pl.BlockSpec(memory_space=pltpu.VMEM)] * 2,
        out_shape=[
            jax.ShapeDtypeStruct((rows, sequences), BF),
            jax.ShapeDtypeStruct((right.shape[1], right.shape[0], sequences), BF),
        ],
        scratch_shapes=[
            pltpu.VMEM((rows, depth), BF),
            pltpu.VMEM((depth, sequences), BF),
            pltpu.SemaphoreType.DMA((pieces,)),
        ],
        compiler_params=pltpu.CompilerParams(vmem_limit_bytes=VMEM),
        cost_estimate=pl.CostEstimate(
            flops=4 * rows * depth * sequences, bytes_accessed=22 << 20, transcendentals=0
        ),
        name="left_grads",
    )(right, grad)


def right_grads(left, grad, columns):
    rows, sequences = left.shape
    depth = grad.shape[1]
    pieces = 10
    return pl.pallas_call(
        functools.partial(right_grad_kernel, pieces),
        in_specs=[
            pl.BlockSpec(memory_space=pltpu.VMEM),
            pl.BlockSpec(memory_space=pl.ANY),
        ],
        out_specs=pl.BlockSpec(memory_space=pltpu.VMEM),
        out_shape=jax.ShapeDtypeStruct((columns, depth // LANES, sequences), BF),
        scratch_shapes=[
            pltpu.VMEM((rows, depth), BF),
            pltpu.VMEM((sequences, depth), F32),
            pltpu.VMEM((columns, depth // LANES, sequences), F32),
            pltpu.SemaphoreType.DMA((pieces,)),
        ],
        compiler_params=pltpu.CompilerParams(vmem_limit_bytes=VMEM),
        cost_estimate=pl.CostEstimate(
            flops=4 * rows * depth * sequences, bytes_accessed=22 << 20, transcendentals=0
        ),
        name="right_grads",
    )(left, grad)


def pairs(left, right, cotangent, weight, offset, width, blocks, pack):
    rows, columns, out = cotangent.shape
    sequences = left.shape[1]
    channels = weight.shape[0]
    group = 20
    depth = right.shape[0]
    return pl.pallas_call(
        functools.partial(pair_kernel, width, group),
        grid=(rows // group,),
        in_specs=[
            pl.BlockSpec((group * width, sequences), lambda i: (i, 0)),
            pl.BlockSpec(right.shape, lambda i: (0, 0, 0)),
            pl.BlockSpec((group, columns, out), lambda i: (i, 0, 0)),
            pl.BlockSpec((channels, out), lambda i: (0, 0)),
            pl.BlockSpec((1, out), lambda i: (0, 0)),
        ],
        out_specs=[
            pl.BlockSpec((group, columns, out), lambda i: (i, 0, 0)),
            pl.BlockSpec((blocks, pack, out), lambda i: (0, 0, 0)),
        ],
        out_shape=[
            jax.ShapeDtypeStruct((rows, columns, out), BF),
            jax.ShapeDtypeStruct((blocks, pack, out), BF),
        ],
        scratch_shapes=[
            pltpu.VMEM((channels, out), F32),
            pltpu.VMEM((out, channels), BF),
            pltpu.VMEM((sequences, depth * LANES), BF),
            pltpu.VMEM((channels, group * LANES), BF),
        ],
        compiler_params=params(),
        cost_estimate=pl.CostEstimate(
            flops=12 * rows * LANES * channels * out, bytes_accessed=6 << 20, transcendentals=0
        ),
        name="pairs",
    )(left, right, cotangent, weight, offset)


def after(value, *others):
    return lax.optimization_barrier((value, *others))[0]


def shards(
    sequence_features,
    first_projection,
    second_projection,
    final_projection,
    final_offset,
    edge_change_cotangent,
):
    n_row = lax.axis_size("row")
    n_col = lax.axis_size("col")
    owned, _, sequences = sequence_features.shape
    rows, columns, out = edge_change_cotangent.shape
    width = first_projection.shape[1]
    scale = 1.0 / sequences

    weight = final_projection.reshape(width, width, out).swapaxes(0, 1).reshape(-1, out)
    channels = weight.shape[0]
    offset = final_offset.reshape(1, out)

    left, right = project(
        sequence_features, first_projection.T, second_projection.T, scale, n_col
    )
    right = swap_axes(right)
    grad, bias_local = outer_grads(edge_change_cotangent, after(weight, left), width)
    left = exchange(left, "col").reshape(rows * width, sequences)

    right = gather_blocks(after(right, bias_local), "row").reshape(columns, width, sequences)

    right_part = right_grads(left, grad, columns)
    left_part, panel = left_grads(after(right, right_part), grad, scale)
    right_sum = scatter_blocks(right_part, "row")

    each = width // n_row
    main = channels // n_row
    pack = -(-(main + each + 1) // 8) * 8
    pair_delta, total = pairs(
        left, panel, edge_change_cotangent, weight, after(offset, left_part, right_sum), width,
        n_row, pack,
    )
    left_sum = scatter_blocks(left_part.reshape(rows, width, sequences), "col")

    exact = lax.Precision.HIGHEST
    left_weight = jnp.einsum(
        "gph,gah->ap", sequence_features.astype(F32), left_sum, precision=exact
    )
    right_back = swap_axes(right_sum)
    right_weight = jnp.einsum(
        "gph,gah->ap", sequence_features.astype(F32), right_back, precision=exact
    )

    small = jnp.concatenate([left_weight, right_weight], axis=1).reshape(n_row, each, LANES)
    bias = jnp.pad(bias_local[:1][None], ((0, n_row - 1), (0, 0), (0, 0)))
    small = jnp.concatenate([small, bias], axis=1).astype(BF)
    total = total + jnp.pad(small, ((0, 0), (main, pack - main - each - 1), (0, 0)))
    total = scatter_blocks(total.reshape(n_row * pack, out), "row").astype(BF)
    alignment_gradient = jnp.einsum(
        "awr,iw->air", left_sum, first_projection.astype(F32), precision=exact
    ) + jnp.einsum("awr,iw->air", right_back, second_projection.astype(F32), precision=exact)
    total = jnp.sum(gather_blocks(total, "col").astype(F32), axis=0).astype(BF)
    total = gather_blocks(total, "row")
    total, left_weight, right_weight, bias = unpack(
        total, width, left_weight.shape[1], 1.0 / (owned * n_row * n_col)
    )
    return (
        pair_delta,
        alignment_gradient,
        left_weight.T,
        right_weight.T,
        total.reshape(channels, out),
        bias.reshape(out),
    )


def solution(mesh):
    placed = (P(("row", "col"), None, None), P(), P(), P(), P(), P("row", "col", None))
    return jax.shard_map(
        shards,
        mesh=mesh,
        in_specs=placed,
        out_specs=(P("row", "col", None), P(("row", "col"), None, None), P(), P(), P(), P()),
        check_vma=False,
    )
```

time: 159 us -> 150 us (0.943)
  the two profiles are of different devices: /device:TPU:38 before, /device:TPU:1 now
where the time goes in v1:
time: 150 us; the launch traced here: 149 us
  Pallas kernels  49.5 us (33%)
  starting transfers between devices  48.1 us (32%)
  blocking collectives  31.8 us (21%)
  waiting for transfers between devices  10.3 us (7%)
  local copies, waits for them, and re-layouts  5.91 us (4%)
  matrix products  1.63 us (1%)
    all_to_all x5, starting transfers between devices, exchange(): return lax.all_to_all(x, axis, 0, 0, tiled=True)  37.4 us
    all_to_all x2, blocking collectives, exchange(): return lax.all_to_all(x, axis, 0, 0, tiled=True)  31.8 us
    pallas_call x1, Pallas kernels, pairs(): pl.pallas_call(functools.partial(pair_kernel, width, group), grid=(rows /...  17.1 us
    ppermute x2, starting transfers between devices, swap_axes(): lax.ppermute(x, ('row', 'col'), [(r * n + c, c * n + r) for r in range(n)...  10.7 us
    pallas_call x1, Pallas kernels, left_grads(): pl.pallas_call(functools.partial(left_grad_kernel, scale, pieces), in_spe...  10.6 us
    pallas_call x1, Pallas kernels, right_grads(): pl.pallas_call(functools.partial(right_grad_kernel, pieces), in_specs=[pl...  9.92 us
    pallas_call x1, Pallas kernels, outer_grads(): pl.pallas_call(functools.partial(outer_grad_kernel, width, pieces), in_sp...  9.87 us
    all_to_all x5, waiting for transfers between devices, exchange(): return lax.all_to_all(x, axis, 0, 0, tiled=True)  9.4 us
  transfers between devices with their start and end apart: 7, of which 5 were waited for; matrix products, arithmetic and copies ran while one was open for 2% of the time, Pallas kernels for 32%

profile of v1, /device:TPU:1, one launch (start us, length us, event | category | flops | bytes accessed | tf_op | source)
XLA Modules:
  0.0 149.4 jit_solution(2404514499492568342)
XLA Ops:
  0.6 0.0 copy-start
  0.6 0.9 copy-done
  1.5 0.0 copy-start.2
  1.5 0.7 copy-done.2
  2.2 0.0 copy-start.4
  2.2 0.7 copy-done.4
  2.9 1.0 project.1
  3.9 11.7 %all-to-all-start = ((bf16[16,5,32,128]{3,2,1,0:T(8,128)(2,1)}), bf16[16,5,32,128]{3,2,1,0:T(8,128)(2,1)S(1)}, u32[]{:S(2)}, u32[]{:S(2)}) async-start(bf16[16,5,32,128]{3,2,1,0:T(8,128)(2,1)} %get-tuple-element.22), calls=%async_computation | async-start | bytes 1310720 | tf_op jit(solution)/shard_map/all_to_all | solution.py:17
  15.7 5.3 %collective-permute-start = (bf16[5,32,128]{2,1,0:T(8,128)(2,1)S(1)}, bf16[5,32,128]{2,1,0:T(8,128)(2,1)S(1)}, u32[]{:S(2)}, u32[]{:S(2)}) collective-permute-start(bf16[5,32,128]{2,1,0:T(8,128)(2,1)S(1)} %get-tuple-element.23), channel_id=1, source_target_pairs={{0,0},{1,16},{2,32},{3,48},{4,64},{5,80},{6,96},{7,112},{8,128},{9... | collective-permute-start | bytes 122888 | tf_op jit(solution)/shard_map/ppermute | solution.py:32
  21.0 1.8 %copy.13 = bf16[32,32,128]{2,0,1:T(8,128)(2,1)} copy(bf16[32,32,128]{2,1,0:T(8,128)(2,1)} %bitcast.47) | data formatting | bytes 524288 | tf_op jit(solution)/shard_map/reshape | solution.py:361
  22.8 9.9 %outer_grads.1 = (bf16[2560,4096]{1,0:T(8,128)(2,1)}, f32[8,128]{1,0:T(8,128)}) custom-call(bf16[80,80,128]{2,1,0:T(8,128)(2,1)} %t_ref.3, bf16[1024,128]{1,0:T(8,128)(2,1)} %bitcast.48), custom_call_target="tpu_custom_call" | custom-call | flops 3355443200 | bytes 23068672 | tf_op jit(solution)/shard_map/outer_grads/pallas_call | solution.py:227
  32.6 0.9 collective-permute-done
  33.5 1.2 all-to-all-done
  34.7 0.0 copy-start.6
  34.7 1.0 broadcast_in_dim.9
  35.7 10.5 %all-to-all-start.1 = ((bf16[16,5,32,128]{3,2,1,0:T(8,128)(2,1)}), bf16[16,5,32,128]{3,2,1,0:T(8,128)(2,1)S(1)}, u32[]{:S(2)}, u32[]{:S(2)}) async-start(bf16[16,5,32,128]{3,2,1,0:T(8,128)(2,1)} %broadcast_in_dim.9), calls=%async_computation.1 | async-start | bytes 1310720 | tf_op jit(solution)/shard_map/all_to_all | solution.py:17
  46.3 0.0 copy-done.6
  46.3 0.0 copy-start.8
  46.3 9.9 %right_grads.1 = bf16[80,32,128]{2,1,0:T(8,128)(2,1)} custom-call(bf16[2560,128]{1,0:T(8,128)(2,1)} %bitcast.42, bf16[2560,4096]{1,0:T(8,128)(2,1)} %get-tuple-element.27.g_ref), custom_call_target="tpu_custom_call" | custom-call | flops 5368709120 | bytes 23068672 | tf_op jit(solution)/shard_map/right_grads/pallas_call | solution.py:282
  56.2 1.3 all-to-all-done.1
  57.5 0.0 copy-start.7
  57.5 4.5 %all-to-all-start.2 = ((bf16[16,5,32,128]{3,2,1,0:T(8,128)(2,1)}), bf16[16,5,32,128]{3,2,1,0:T(8,128)(2,1)S(1)}, u32[]{:S(2)}, u32[]{:S(2)}) async-start(bf16[16,5,32,128]{3,2,1,0:T(8,128)(2,1)} %bitcast.44), calls=%async_computation.2 | async-start | bytes 1310720 | tf_op jit(solution)/shard_map/all_to_all | solution.py:17
  62.1 0.0 copy-done.8
  62.1 0.0 copy-done.7
  62.1 10.6 %left_grads.1 = (bf16[2560,128]{1,0:T(8,128)(2,1)}, bf16[32,80,128]{2,1,0:T(8,128)(2,1)}) custom-call(bf16[80,32,128]{2,1,0:T(8,128)(2,1)} %bitcast.45, bf16[2560,4096]{1,0:T(8,128)(2,1)} %get-tuple-element.27.g_ref), custom_call_target="tpu_custom_call" | custom-call | flops 5368709120 | bytes 23068672 | tf_op jit(solution)/shard_map/left_grads/pallas_call | solution.py:254
  72.7 0.7 all-to-all-done.2
  73.4 3.6 %all-to-all-start.3 = ((bf16[16,5,32,128]{3,2,1,0:T(8,128)(2,1)}), bf16[16,5,32,128]{3,2,1,0:T(8,128)(2,1)S(1)}, u32[]{:S(2)}, u32[]{:S(2)}) async-start(bf16[16,5,32,128]{3,2,1,0:T(8,128)(2,1)} %bitcast.46), calls=%async_computation.3 | async-start | bytes 1310720 | tf_op jit(solution)/shard_map/all_to_all | solution.py:17
  77.0 0.1 convert_reduce_fusion.1
  77.1 5.4 %collective-permute-start.1 = (f32[5,32,128]{2,1,0:T(8,128)S(1)}, f32[5,32,128]{2,1,0:T(8,128)S(1)}, u32[]{:S(2)}, u32[]{:S(2)}) collective-permute-start(f32[5,32,128]{2,1,0:T(8,128)S(1)} %convert_reduce_fusion.1), channel_id=1, source_target_pairs={{0,0},{1,16},{2,32},{3,48},{4,64},{5,80},{6,96},{7,112},{8,128},{9... | collective-permute-start | bytes 245768 | tf_op jit(solution)/shard_map/ppermute | solution.py:32
  82.5 0.0 copy-start.1
  82.5 17.1 %pairs.1 = (bf16[80,80,128]{2,1,0:T(8,128)(2,1)}, bf16[16,72,128]{2,1,0:T(8,128)(2,1)}) custom-call(bf16[2560,128]{1,0:T(8,128)(2,1)} %bitcast.43, bf16[32,80,128]{2,1,0:T(8,128)(2,1)} %get-tuple-element.29.r_ref, bf16[80,80,128]{2,1,0:T(8,128)(2,1)} %t_ref.3, bf16[1024,128]{1,0:T(8,128)(2,1)} %bitcast.49, f32[1,128]{1,0:T(1,128)} %bitcast.54), custom_call_target="tpu_custom_call" | custom-call | flops 16106127360 | bytes 6291456 | tf_op jit(solution)/shard_map/pairs/pallas_call | solution.py:310
  99.6 0.0 all-to-all-done.3
  99.6 0.1 convert_reduce_fusion
  99.7 0.0 copy-done.1
  99.7 0.2 fusion.1
  99.9 0.0 collective-permute-done.1
  99.9 0.2 fusion.2
  100.1 0.1 pad_maximum_fusion
  100.2 1.0 pad_add_fusion
  101.2 0.0 copy-start.3
  101.2 0.0 copy-start.5
  101.3 17.3 %all_to_all.35 = bf16[16,72,128]{2,1,0:T(8,128)(2,1)S(1)} all-to-all(bf16[16,72,128]{2,1,0:T(8,128)(2,1)S(1)} %pad_add_fusion), channel_id=1, replica_groups=mesh['row'=16,'col'=16] {'row'}, dimensions={0} | all-to-all | bytes 589824 | tf_op jit(solution)/shard_map/all_to_all | solution.py:17
  118.7 14.5 %all_to_all.36 = bf16[16,72,128]{2,1,0:T(8,128)(2,1)S(1)} all-to-all(bf16[16,72,128]{2,1,0:T(8,128)(2,1)S(1)} %broadcast_in_dim.11), channel_id=1, replica_groups=mesh['row'=16,'col'=16] {'col'}, dimensions={0} | all-to-all | bytes 589824 | tf_op jit(solution)/shard_map/all_to_all | solution.py:17
  133.2 0.8 broadcast_in_dim.12
  134.0 7.0 %all-to-all-start.6 = ((bf16[16,72,128]{2,1,0:T(8,128)(2,1)}), bf16[16,72,128]{2,1,0:T(8,128)(2,1)S(1)}, u32[]{:S(2)}, u32[]{:S(2)}) async-start(bf16[16,72,128]{2,1,0:T(8,128)(2,1)} %broadcast_in_dim.12), calls=%async_computation.6 | async-start | bytes 589824 | tf_op jit(solution)/shard_map/all_to_all | solution.py:17
  141.0 0.0 copy-done.3
  141.0 0.3 fusion.6
  141.2 0.0 copy-done.5
  141.2 0.9 fusion
  142.2 6.2 %all-to-all-done.6.pack_ref = bf16[16,72,128]{2,1,0:T(8,128)(2,1)S(1)} async-done(((bf16[16,72,128]{2,1,0:T(8,128)(2,1)}), bf16[16,72,128]{2,1,0:T(8,128)(2,1)S(1)}, u32[]{:S(2)}, u32[]{:S(2)}) %all-to-all-start.6) | async-done | bytes 294944 | tf_op jit(solution)/shard_map/all_to_all | solution.py:17
  148.4 1.0 unpack.1
  (6 shorter events, 0.2 us)
Async XLA Ops:
  0.6 0.9 copy-start
  1.5 0.7 copy-start.2
  2.2 0.7 copy-start.4
  3.9 30.8 %all-to-all-start = ((bf16[16,5,32,128]{3,2,1,0:T(8,128)(2,1)}), bf16[16,5,32,128]{3,2,1,0:T(8,128)(2,1)S(1)}, u32[]{:S(2)}, u32[]{:S(2)}) async-start(bf16[16,5,32,128]{3,2,1,0:T(8,128)(2,1)} %get-tuple-element.22), calls=%async_computation | async-start | bytes 1310720 | tf_op jit(solution)/shard_map/all_to_all | solution.py:17
  15.7 17.8 %collective-permute-start = (bf16[5,32,128]{2,1,0:T(8,128)(2,1)S(1)}, bf16[5,32,128]{2,1,0:T(8,128)(2,1)S(1)}, u32[]{:S(2)}, u32[]{:S(2)}) collective-permute-start(bf16[5,32,128]{2,1,0:T(8,128)(2,1)S(1)} %get-tuple-element.23), channel_id=1, source_target_pairs={{0,0},{1,16},{2,32},{3,48},{4,64},{5,80},{6,96},{7,112},{8,128},{9... | collective-permute-start | bytes 122888 | tf_op jit(solution)/shard_map/ppermute | solution.py:32
  34.7 11.6 %copy-start.6 = (bf16[16,5,32,128]{3,2,1,0:T(8,128)(2,1)}, bf16[16,5,32,128]{3,2,1,0:T(8,128)(2,1)S(1)}, u32[]{:S(2)}) copy-start(bf16[16,5,32,128]{3,2,1,0:T(8,128)(2,1)S(1)} %all-to-all-done) | copy-start | bytes 1966084
  35.7 21.8 %all-to-all-start.1 = ((bf16[16,5,32,128]{3,2,1,0:T(8,128)(2,1)}), bf16[16,5,32,128]{3,2,1,0:T(8,128)(2,1)S(1)}, u32[]{:S(2)}, u32[]{:S(2)}) async-start(bf16[16,5,32,128]{3,2,1,0:T(8,128)(2,1)} %broadcast_in_dim.9), calls=%async_computation.1 | async-start | bytes 1310720 | tf_op jit(solution)/shard_map/all_to_all | solution.py:17
  46.3 15.8 %copy-start.8 = (f32[8,128]{1,0:T(8,128)S(1)}, f32[8,128]{1,0:T(8,128)}, u32[]{:S(2)}) copy-start(f32[8,128]{1,0:T(8,128)} %get-tuple-element.25) | copy-start | bytes 12292
  57.5 4.6 %copy-start.7 = (bf16[16,5,32,128]{3,2,1,0:T(8,128)(2,1)}, bf16[16,5,32,128]{3,2,1,0:T(8,128)(2,1)S(1)}, u32[]{:S(2)}) copy-start(bf16[16,5,32,128]{3,2,1,0:T(8,128)(2,1)S(1)} %all-to-all-done.1) | copy-start | bytes 1966084
  57.5 15.9 %all-to-all-start.2 = ((bf16[16,5,32,128]{3,2,1,0:T(8,128)(2,1)}), bf16[16,5,32,128]{3,2,1,0:T(8,128)(2,1)S(1)}, u32[]{:S(2)}, u32[]{:S(2)}) async-start(bf16[16,5,32,128]{3,2,1,0:T(8,128)(2,1)} %bitcast.44), calls=%async_computation.2 | async-start | bytes 1310720 | tf_op jit(solution)/shard_map/all_to_all | solution.py:17
  73.4 26.2 %all-to-all-start.3 = ((bf16[16,5,32,128]{3,2,1,0:T(8,128)(2,1)}), bf16[16,5,32,128]{3,2,1,0:T(8,128)(2,1)S(1)}, u32[]{:S(2)}, u32[]{:S(2)}) async-start(bf16[16,5,32,128]{3,2,1,0:T(8,128)(2,1)} %bitcast.46), calls=%async_computation.3 | async-start | bytes 1310720 | tf_op jit(solution)/shard_map/all_to_all | solution.py:17
  77.1 22.8 %collective-permute-start.1 = (f32[5,32,128]{2,1,0:T(8,128)S(1)}, f32[5,32,128]{2,1,0:T(8,128)S(1)}, u32[]{:S(2)}, u32[]{:S(2)}) collective-permute-start(f32[5,32,128]{2,1,0:T(8,128)S(1)} %convert_reduce_fusion.1), channel_id=1, source_target_pairs={{0,0},{1,16},{2,32},{3,48},{4,64},{5,80},{6,96},{7,112},{8,128},{9... | collective-permute-start | bytes 245768 | tf_op jit(solution)/shard_map/ppermute | solution.py:32
  82.5 17.2 %copy-start.1 = (bf16[5,64,128]{2,1,0:T(8,128)(2,1)S(1)}, bf16[5,64,128]{2,1,0:T(8,128)(2,1)}, u32[]{:S(2)}) copy-start(bf16[5,64,128]{2,1,0:T(8,128)(2,1)} %x_ref.1) | copy-start | bytes 245764
  101.2 39.7 %copy-start.3 = (bf16[64,32]{0,1:T(8,128)(2,1)S(1)}, bf16[64,32]{0,1:T(8,128)(2,1)}, u32[]{:S(2)}) copy-start(bf16[64,32]{0,1:T(8,128)(2,1)} %param.7) | copy-start | bytes 12292
  101.2 40.0 %copy-start.5 = (bf16[64,32]{0,1:T(8,128)(2,1)S(1)}, bf16[64,32]{0,1:T(8,128)(2,1)}, u32[]{:S(2)}) copy-start(bf16[64,32]{0,1:T(8,128)(2,1)} %param.8) | copy-start | bytes 12292
  134.0 14.4 %all-to-all-start.6 = ((bf16[16,72,128]{2,1,0:T(8,128)(2,1)}), bf16[16,72,128]{2,1,0:T(8,128)(2,1)S(1)}, u32[]{:S(2)}, u32[]{:S(2)}) async-start(bf16[16,72,128]{2,1,0:T(8,128)(2,1)} %broadcast_in_dim.12), calls=%async_computation.6 | async-start | bytes 589824 | tf_op jit(solution)/shard_map/all_to_all | solution.py:17

commit v2 on v1

--- a/solution.py
+++ b/solution.py
@@ -53,7 +53,7 @@
             jax.ShapeDtypeStruct((copies, owned, width, sequences), BF),
             jax.ShapeDtypeStruct((owned, width, sequences), BF),
         ],
-        compiler_params=pltpu.CompilerParams(vmem_limit_bytes=16 << 20),
+        compiler_params=pltpu.CompilerParams(vmem_limit_bytes=VMEM),
         cost_estimate=pl.CostEstimate(flops=1 << 22, bytes_accessed=1 << 20, transcendentals=0),
         name="project",
     )(source, first, second)
@@ -95,8 +95,12 @@
     return jnp.concatenate([t, jnp.zeros((rows - t.shape[0], t.shape[1]), t.dtype)], axis=0)
 
 
-def outer_grad_kernel(width, pieces, t_ref, w_ref, g_ref, bias_ref, buf_ref, sem_ref):
+def outer_grad_kernel(
+    width, pieces, t_ref, natural_ref, g_ref, bias_ref, w_ref, buf_ref, sem_ref
+):
     channels = w_ref.shape[0]
+    swapped = jnp.swapaxes(natural_ref[...].astype(F32), 0, 1)
+    w_ref[...] = swapped.reshape(w_ref.shape).astype(BF)
     group = t_ref.shape[0] // pieces
     total = jnp.zeros((1, LANES), F32)
     copies = []
@@ -222,7 +226,7 @@
 def outer_grads(cotangent, weight, width):
     rows, columns, out = cotangent.shape
     pieces = 10
-    channels = weight.shape[0]
+    channels = weight.shape[0] * weight.shape[1]
     depth = channels // width
     return pl.pallas_call(
         functools.partial(outer_grad_kernel, width, pieces),
@@ -230,10 +234,12 @@
         out_specs=[
             pl.BlockSpec(memory_space=pl.ANY),
             pl.BlockSpec(memory_space=pltpu.VMEM),
+            pl.BlockSpec(memory_space=pltpu.VMEM),
         ],
         out_shape=[
             jax.ShapeDtypeStruct((rows * width, depth * LANES), BF),
             jax.ShapeDtypeStruct((8, out), F32),
+            jax.ShapeDtypeStruct((channels, out), BF),
         ],
         scratch_shapes=[
             pltpu.VMEM((rows * width, depth * LANES), BF),
@@ -358,15 +364,17 @@
     width = first_projection.shape[1]
     scale = 1.0 / sequences
 
-    weight = final_projection.reshape(width, width, out).swapaxes(0, 1).reshape(-1, out)
-    channels = weight.shape[0]
+    channels = final_projection.shape[0]
+    weight = final_projection.reshape(width, width, out)
     offset = final_offset.reshape(1, out)
 
     left, right = project(
         sequence_features, first_projection.T, second_projection.T, scale, n_col
     )
     right = swap_axes(right)
-    grad, bias_local = outer_grads(edge_change_cotangent, after(weight, left), width)
+    grad, bias_local, weight = outer_grads(
+        edge_change_cotangent, after(weight, left), width
+    )
     left = exchange(left, "col").reshape(rows * width, sequences)
 
     right = gather_blocks(after(right, bias_local), "row").reshape(columns, width, sequences)

time: 150 us -> 149 us (level)
  local copies, waits for them, and re-layouts: 5.91 us -> 1.86 us
  Pallas kernels: 49.5 us -> 51 us
    unnamed x18 -> x12, local copies, waits for them, and re-layouts: 2.31 us -> 0.03 us
    reshape x1 -> x0, local copies, waits for them, and re-layouts: 1.78 us -> none  [shards(): final_projection.reshape(width, width, out).swapaxes(0, 1).reshape(-1, out)]
  transfers between devices with their start and end apart: 7 -> 7, of which waited for: 5 -> 5; matrix products, arithmetic and copies ran while one was open for 2% -> 1% of each run, Pallas kernels for 32% -> 33%
where the time goes in v2:
time: 149 us; the launch traced here: 148 us
  Pallas kernels  51 us (34%)
  starting transfers between devices  48.1 us (32%)
  blocking collectives  31.8 us (21%)
  waiting for transfers between devices  11.4 us (8%)
  local copies, waits for them, and re-layouts  1.86 us (1%)
  matrix products  1.63 us (1%)
    all_to_all x5, starting transfers between devices, exchange(): return lax.all_to_all(x, axis, 0, 0, tiled=True)  37.4 us
    all_to_all x2, blocking collectives, exchange(): return lax.all_to_all(x, axis, 0, 0, tiled=True)  31.8 us
    pallas_call x1, Pallas kernels, pairs(): pl.pallas_call(functools.partial(pair_kernel, width, group), grid=(rows /...  17.1 us
    ppermute x2, starting transfers between devices, swap_axes(): lax.ppermute(x, ('row', 'col'), [(r * n + c, c * n + r) for r in range(n)...  10.7 us
    pallas_call x1, Pallas kernels, left_grads(): pl.pallas_call(functools.partial(left_grad_kernel, scale, pieces), in_spe...  10.6 us
    pallas_call x1, Pallas kernels, outer_grads(): pl.pallas_call(functools.partial(outer_grad_kernel, width, pieces), in_sp...  10.5 us
    pallas_call x1, Pallas kernels, right_grads(): pl.pallas_call(functools.partial(right_grad_kernel, pieces), in_specs=[pl...  9.93 us
    all_to_all x5, waiting for transfers between devices, exchange(): return lax.all_to_all(x, axis, 0, 0, tiled=True)  9.39 us
  transfers between devices with their start and end apart: 7, of which 5 were waited for; matrix products, arithmetic and copies ran while one was open for 1% of the time, Pallas kernels for 33%

profile of v2, /device:TPU:1, one launch (start us, length us, event | category | flops | bytes accessed | tf_op | source)
XLA Modules:
  0.0 148.0 jit_solution(15286856014106926527)
XLA Ops:
  0.6 1.9 %project.1 = (bf16[16,5,32,128]{3,2,1,0:T(8,128)(2,1)}, bf16[5,32,128]{2,1,0:T(8,128)(2,1)}) custom-call(bf16[5,64,128]{2,1,0:T(8,128)(2,1)} %x_ref.1, bf16[32,64]{1,0:T(8,128)(2,1)} %bitcast.42, bf16[32,64]{1,0:T(8,128)(2,1)} %bitcast.43), custom_call_target="tpu_custom_call" | custom-call | flops 4194304 | bytes 1048576 | tf_op jit(solution)/shard_map/project/pallas_call | solution.py:50
  2.6 11.7 %all-to-all-start = ((bf16[16,5,32,128]{3,2,1,0:T(8,128)(2,1)}), bf16[16,5,32,128]{3,2,1,0:T(8,128)(2,1)S(1)}, u32[]{:S(2)}, u32[]{:S(2)}) async-start(bf16[16,5,32,128]{3,2,1,0:T(8,128)(2,1)} %get-tuple-element.23), calls=%async_computation | async-start | bytes 1310720 | tf_op jit(solution)/shard_map/all_to_all | solution.py:17
  14.3 5.3 %collective-permute-start = (bf16[5,32,128]{2,1,0:T(8,128)(2,1)}, bf16[5,32,128]{2,1,0:T(8,128)(2,1)S(1)}, u32[]{:S(2)}, u32[]{:S(2)}) collective-permute-start(bf16[5,32,128]{2,1,0:T(8,128)(2,1)} %get-tuple-element.24), channel_id=1, source_target_pairs={{0,0},{1,16},{2,32},{3,48},{4,64},{5,80},{6,96},{7,112},{8,128},{9... | collective-permute-start | bytes 122888 | tf_op jit(solution)/shard_map/ppermute | solution.py:32
  19.6 10.5 %outer_grads.1 = (bf16[2560,4096]{1,0:T(8,128)(2,1)}, f32[8,128]{1,0:T(8,128)}, bf16[1024,128]{1,0:T(8,128)(2,1)}) custom-call(bf16[80,80,128]{2,1,0:T(8,128)(2,1)} %t_ref.3, bf16[32,32,128]{2,1,0:T(8,128)(2,1)} %bitcast.46), custom_call_target="tpu_custom_call" | custom-call | flops 3355443200 | bytes 23068672 | tf_op jit(solution)/shard_map/outer_grads/pallas_call | solution.py:231
  30.1 2.0 %collective-permute-done = bf16[5,32,128]{2,1,0:T(8,128)(2,1)S(1)} collective-permute-done((bf16[5,32,128]{2,1,0:T(8,128)(2,1)}, bf16[5,32,128]{2,1,0:T(8,128)(2,1)S(1)}, u32[]{:S(2)}, u32[]{:S(2)}) %collective-permute-start) | collective-permute-done | bytes 40992 | tf_op jit(solution)/shard_map/ppermute | solution.py:32
  32.1 1.2 all-to-all-done
  33.3 0.0 copy-start
  33.3 1.0 broadcast_in_dim.9
  34.4 10.5 %all-to-all-start.1 = ((bf16[16,5,32,128]{3,2,1,0:T(8,128)(2,1)}), bf16[16,5,32,128]{3,2,1,0:T(8,128)(2,1)S(1)}, u32[]{:S(2)}, u32[]{:S(2)}) async-start(bf16[16,5,32,128]{3,2,1,0:T(8,128)(2,1)} %broadcast_in_dim.9), calls=%async_computation.1 | async-start | bytes 1310720 | tf_op jit(solution)/shard_map/all_to_all | solution.py:17
  44.9 0.0 copy-done
  44.9 0.0 copy-start.5
  44.9 9.9 %right_grads.1 = bf16[80,32,128]{2,1,0:T(8,128)(2,1)} custom-call(bf16[2560,128]{1,0:T(8,128)(2,1)} %bitcast.37, bf16[2560,4096]{1,0:T(8,128)(2,1)} %get-tuple-element.28.g_ref), custom_call_target="tpu_custom_call" | custom-call | flops 5368709120 | bytes 23068672 | tf_op jit(solution)/shard_map/right_grads/pallas_call | solution.py:288
  54.9 1.3 all-to-all-done.1
  56.1 0.0 copy-start.1
  56.1 4.5 %all-to-all-start.2 = ((bf16[16,5,32,128]{3,2,1,0:T(8,128)(2,1)}), bf16[16,5,32,128]{3,2,1,0:T(8,128)(2,1)S(1)}, u32[]{:S(2)}, u32[]{:S(2)}) async-start(bf16[16,5,32,128]{3,2,1,0:T(8,128)(2,1)} %bitcast.39), calls=%async_computation.2 | async-start | bytes 1310720 | tf_op jit(solution)/shard_map/all_to_all | solution.py:17
  60.7 0.0 copy-done.5
  60.7 0.0 copy-done.1
  60.7 10.6 %left_grads.1 = (bf16[2560,128]{1,0:T(8,128)(2,1)}, bf16[32,80,128]{2,1,0:T(8,128)(2,1)}) custom-call(bf16[80,32,128]{2,1,0:T(8,128)(2,1)} %bitcast.40, bf16[2560,4096]{1,0:T(8,128)(2,1)} %get-tuple-element.28.g_ref), custom_call_target="tpu_custom_call" | custom-call | flops 5368709120 | bytes 23068672 | tf_op jit(solution)/shard_map/left_grads/pallas_call | solution.py:260
  71.3 0.7 all-to-all-done.2
  72.0 3.6 %all-to-all-start.3 = ((bf16[16,5,32,128]{3,2,1,0:T(8,128)(2,1)}), bf16[16,5,32,128]{3,2,1,0:T(8,128)(2,1)S(1)}, u32[]{:S(2)}, u32[]{:S(2)}) async-start(bf16[16,5,32,128]{3,2,1,0:T(8,128)(2,1)} %bitcast.41), calls=%async_computation.3 | async-start | bytes 1310720 | tf_op jit(solution)/shard_map/all_to_all | solution.py:17
  75.6 0.1 convert_reduce_fusion.1
  75.7 5.4 %collective-permute-start.1 = (f32[5,32,128]{2,1,0:T(8,128)S(1)}, f32[5,32,128]{2,1,0:T(8,128)S(1)}, u32[]{:S(2)}, u32[]{:S(2)}) collective-permute-start(f32[5,32,128]{2,1,0:T(8,128)S(1)} %convert_reduce_fusion.1), channel_id=1, source_target_pairs={{0,0},{1,16},{2,32},{3,48},{4,64},{5,80},{6,96},{7,112},{8,128},{9... | collective-permute-start | bytes 245768 | tf_op jit(solution)/shard_map/ppermute | solution.py:32
  81.1 0.0 copy-start.2
  81.1 17.1 %pairs.1 = (bf16[80,80,128]{2,1,0:T(8,128)(2,1)}, bf16[16,72,128]{2,1,0:T(8,128)(2,1)}) custom-call(bf16[2560,128]{1,0:T(8,128)(2,1)} %bitcast.38, bf16[32,80,128]{2,1,0:T(8,128)(2,1)} %get-tuple-element.30.r_ref, bf16[80,80,128]{2,1,0:T(8,128)(2,1)} %t_ref.3, bf16[1024,128]{1,0:T(8,128)(2,1)} %get-tuple-element.31.w_ref, f32[1,128]{1,0:T(1,128)} %bitcast.49), custom_call_target="tpu_custom_call" | custom-call | flops 16106127360 | bytes 6291456 | tf_op jit(solution)/shard_map/pairs/pallas_call | solution.py:316
  98.2 0.0 all-to-all-done.3
  98.2 0.1 convert_reduce_fusion
  98.3 0.0 copy-done.2
  98.3 0.2 fusion.1
  98.5 0.0 collective-permute-done.1
  98.6 0.2 fusion.2
  98.8 0.1 pad_maximum_fusion
  98.9 1.0 pad_add_fusion
  99.9 0.0 copy-start.3
  99.9 0.0 copy-start.4
  99.9 17.3 %all_to_all.35 = bf16[16,72,128]{2,1,0:T(8,128)(2,1)S(1)} all-to-all(bf16[16,72,128]{2,1,0:T(8,128)(2,1)S(1)} %pad_add_fusion), channel_id=1, replica_groups=mesh['row'=16,'col'=16] {'row'}, dimensions={0} | all-to-all | bytes 589824 | tf_op jit(solution)/shard_map/all_to_all | solution.py:17
  117.3 14.5 %all_to_all.36 = bf16[16,72,128]{2,1,0:T(8,128)(2,1)S(1)} all-to-all(bf16[16,72,128]{2,1,0:T(8,128)(2,1)S(1)} %broadcast_in_dim.11), channel_id=1, replica_groups=mesh['row'=16,'col'=16] {'col'}, dimensions={0} | all-to-all | bytes 589824 | tf_op jit(solution)/shard_map/all_to_all | solution.py:17
  131.9 0.8 broadcast_in_dim.12
  132.6 7.0 %all-to-all-start.6 = ((bf16[16,72,128]{2,1,0:T(8,128)(2,1)}), bf16[16,72,128]{2,1,0:T(8,128)(2,1)S(1)}, u32[]{:S(2)}, u32[]{:S(2)}) async-start(bf16[16,72,128]{2,1,0:T(8,128)(2,1)} %broadcast_in_dim.12), calls=%async_computation.6 | async-start | bytes 589824 | tf_op jit(solution)/shard_map/all_to_all | solution.py:17
  139.6 0.0 copy-done.3
  139.6 0.3 fusion.6
  139.9 0.0 copy-done.4
  139.9 0.9 fusion
  140.8 6.2 %all-to-all-done.6.pack_ref = bf16[16,72,128]{2,1,0:T(8,128)(2,1)S(1)} async-done(((bf16[16,72,128]{2,1,0:T(8,128)(2,1)}), bf16[16,72,128]{2,1,0:T(8,128)(2,1)S(1)}, u32[]{:S(2)}, u32[]{:S(2)}) %all-to-all-start.6) | async-done | bytes 294944 | tf_op jit(solution)/shard_map/all_to_all | solution.py:17
  147.0 1.0 unpack.1
  (6 shorter events, 0.2 us)
Async XLA Ops:
  2.6 30.8 %all-to-all-start = ((bf16[16,5,32,128]{3,2,1,0:T(8,128)(2,1)}), bf16[16,5,32,128]{3,2,1,0:T(8,128)(2,1)S(1)}, u32[]{:S(2)}, u32[]{:S(2)}) async-start(bf16[16,5,32,128]{3,2,1,0:T(8,128)(2,1)} %get-tuple-element.23), calls=%async_computation | async-start | bytes 1310720 | tf_op jit(solution)/shard_map/all_to_all | solution.py:17
  14.3 17.8 %collective-permute-start = (bf16[5,32,128]{2,1,0:T(8,128)(2,1)}, bf16[5,32,128]{2,1,0:T(8,128)(2,1)S(1)}, u32[]{:S(2)}, u32[]{:S(2)}) collective-permute-start(bf16[5,32,128]{2,1,0:T(8,128)(2,1)} %get-tuple-element.24), channel_id=1, source_target_pairs={{0,0},{1,16},{2,32},{3,48},{4,64},{5,80},{6,96},{7,112},{8,128},{9... | collective-permute-start | bytes 122888 | tf_op jit(solution)/shard_map/ppermute | solution.py:32
  33.3 11.6 %copy-start = (bf16[16,5,32,128]{3,2,1,0:T(8,128)(2,1)}, bf16[16,5,32,128]{3,2,1,0:T(8,128)(2,1)S(1)}, u32[]{:S(2)}) copy-start(bf16[16,5,32,128]{3,2,1,0:T(8,128)(2,1)S(1)} %all-to-all-done) | copy-start | bytes 1966084
  34.4 21.8 %all-to-all-start.1 = ((bf16[16,5,32,128]{3,2,1,0:T(8,128)(2,1)}), bf16[16,5,32,128]{3,2,1,0:T(8,128)(2,1)S(1)}, u32[]{:S(2)}, u32[]{:S(2)}) async-start(bf16[16,5,32,128]{3,2,1,0:T(8,128)(2,1)} %broadcast_in_dim.9), calls=%async_computation.1 | async-start | bytes 1310720 | tf_op jit(solution)/shard_map/all_to_all | solution.py:17
  44.9 15.8 %copy-start.5 = (f32[8,128]{1,0:T(8,128)S(1)}, f32[8,128]{1,0:T(8,128)}, u32[]{:S(2)}) copy-start(f32[8,128]{1,0:T(8,128)} %get-tuple-element.26) | copy-start | bytes 12292
  56.1 4.6 %copy-start.1 = (bf16[16,5,32,128]{3,2,1,0:T(8,128)(2,1)}, bf16[16,5,32,128]{3,2,1,0:T(8,128)(2,1)S(1)}, u32[]{:S(2)}) copy-start(bf16[16,5,32,128]{3,2,1,0:T(8,128)(2,1)S(1)} %all-to-all-done.1) | copy-start | bytes 1966084
  56.1 15.9 %all-to-all-start.2 = ((bf16[16,5,32,128]{3,2,1,0:T(8,128)(2,1)}), bf16[16,5,32,128]{3,2,1,0:T(8,128)(2,1)S(1)}, u32[]{:S(2)}, u32[]{:S(2)}) async-start(bf16[16,5,32,128]{3,2,1,0:T(8,128)(2,1)} %bitcast.39), calls=%async_computation.2 | async-start | bytes 1310720 | tf_op jit(solution)/shard_map/all_to_all | solution.py:17
  72.0 26.2 %all-to-all-start.3 = ((bf16[16,5,32,128]{3,2,1,0:T(8,128)(2,1)}), bf16[16,5,32,128]{3,2,1,0:T(8,128)(2,1)S(1)}, u32[]{:S(2)}, u32[]{:S(2)}) async-start(bf16[16,5,32,128]{3,2,1,0:T(8,128)(2,1)} %bitcast.41), calls=%async_computation.3 | async-start | bytes 1310720 | tf_op jit(solution)/shard_map/all_to_all | solution.py:17
  75.7 22.8 %collective-permute-start.1 = (f32[5,32,128]{2,1,0:T(8,128)S(1)}, f32[5,32,128]{2,1,0:T(8,128)S(1)}, u32[]{:S(2)}, u32[]{:S(2)}) collective-permute-start(f32[5,32,128]{2,1,0:T(8,128)S(1)} %convert_reduce_fusion.1), channel_id=1, source_target_pairs={{0,0},{1,16},{2,32},{3,48},{4,64},{5,80},{6,96},{7,112},{8,128},{9... | collective-permute-start | bytes 245768 | tf_op jit(solution)/shard_map/ppermute | solution.py:32
  81.1 17.2 %copy-start.2 = (bf16[5,64,128]{2,1,0:T(8,128)(2,1)S(1)}, bf16[5,64,128]{2,1,0:T(8,128)(2,1)}, u32[]{:S(2)}) copy-start(bf16[5,64,128]{2,1,0:T(8,128)(2,1)} %x_ref.1) | copy-start | bytes 245764
  99.9 39.7 %copy-start.3 = (bf16[64,32]{0,1:T(8,128)(2,1)S(1)}, bf16[64,32]{0,1:T(8,128)(2,1)}, u32[]{:S(2)}) copy-start(bf16[64,32]{0,1:T(8,128)(2,1)} %param.7) | copy-start | bytes 12292
  99.9 40.0 %copy-start.4 = (bf16[64,32]{0,1:T(8,128)(2,1)S(1)}, bf16[64,32]{0,1:T(8,128)(2,1)}, u32[]{:S(2)}) copy-start(bf16[64,32]{0,1:T(8,128)(2,1)} %param.8) | copy-start | bytes 12292
  132.6 14.4 %all-to-all-start.6 = ((bf16[16,72,128]{2,1,0:T(8,128)(2,1)}), bf16[16,72,128]{2,1,0:T(8,128)(2,1)S(1)}, u32[]{:S(2)}, u32[]{:S(2)}) async-start(bf16[16,72,128]{2,1,0:T(8,128)(2,1)} %broadcast_in_dim.12), calls=%async_computation.6 | async-start | bytes 589824 | tf_op jit(solution)/shard_map/all_to_all | solution.py:17

commit v3 on v2

--- a/solution.py
+++ b/solution.py
@@ -11,6 +11,7 @@
 F32 = jnp.float32
 LANES = 128
 VMEM = 56 * 1024 * 1024
+STREAM = 44 * 1024 * 1024
 
 
 def exchange(x, axis):
@@ -64,7 +65,7 @@
     blocks = pack_ref.shape[0]
     main = weight_ref.shape[0] * weight_ref.shape[1] // blocks
     each = width // blocks
-    total = [pack_ref[n].astype(F32) * inverse for n in range(blocks)]
+    total = [pack_ref[n] * inverse for n in range(blocks)]
     weight = jnp.concatenate([t[:main] for t in total], axis=0).reshape(weight_ref.shape)
     weight_ref[...] = jnp.swapaxes(weight, 0, 1)
     half = left_ref.shape[1]
@@ -210,11 +211,7 @@
 
     @pl.when(pl.program_id(0) == pl.num_programs(0) - 1)
     def _():
-        blocks, pack, out = pack_ref.shape
-        main = gw_ref.shape[0] // blocks
-        for n in range(blocks):
-            block = padded_rows(gw_ref[pl.ds(n * main, main)], pack)
-            pack_ref[n] = block.astype(BF)
+        pack_ref[...] = gw_ref[...].astype(BF)
 
 
 def params():
@@ -273,7 +270,7 @@
             pltpu.VMEM((depth, sequences), BF),
             pltpu.SemaphoreType.DMA((pieces,)),
         ],
-        compiler_params=pltpu.CompilerParams(vmem_limit_bytes=VMEM),
+        compiler_params=pltpu.CompilerParams(vmem_limit_bytes=STREAM),
         cost_estimate=pl.CostEstimate(
             flops=4 * rows * depth * sequences, bytes_accessed=22 << 20, transcendentals=0
         ),
@@ -299,7 +296,7 @@
             pltpu.VMEM((columns, depth // LANES, sequences), F32),
             pltpu.SemaphoreType.DMA((pieces,)),
         ],
-        compiler_params=pltpu.CompilerParams(vmem_limit_bytes=VMEM),
+        compiler_params=pltpu.CompilerParams(vmem_limit_bytes=STREAM),
         cost_estimate=pl.CostEstimate(
             flops=4 * rows * depth * sequences, bytes_accessed=22 << 20, transcendentals=0
         ),
@@ -307,7 +304,7 @@
     )(left, grad)
 
 
-def pairs(left, right, cotangent, weight, offset, width, blocks, pack):
+def pairs(left, right, cotangent, weight, offset, width):
     rows, columns, out = cotangent.shape
     sequences = left.shape[1]
     channels = weight.shape[0]
@@ -325,11 +322,11 @@
         ],
         out_specs=[
             pl.BlockSpec((group, columns, out), lambda i: (i, 0, 0)),
-            pl.BlockSpec((blocks, pack, out), lambda i: (0, 0, 0)),
+            pl.BlockSpec((channels, out), lambda i: (0, 0)),
         ],
         out_shape=[
             jax.ShapeDtypeStruct((rows, columns, out), BF),
-            jax.ShapeDtypeStruct((blocks, pack, out), BF),
+            jax.ShapeDtypeStruct((channels, out), BF),
         ],
         scratch_shapes=[
             pltpu.VMEM((channels, out), F32),
@@ -387,8 +384,7 @@
     main = channels // n_row
     pack = -(-(main + each + 1) // 8) * 8
     pair_delta, total = pairs(
-        left, panel, edge_change_cotangent, weight, after(offset, left_part, right_sum), width,
-        n_row, pack,
+        left, panel, edge_change_cotangent, weight, after(offset, left_part, right_sum), width
     )
     left_sum = scatter_blocks(left_part.reshape(rows, width, sequences), "col")
 
@@ -403,14 +399,15 @@
 
     small = jnp.concatenate([left_weight, right_weight], axis=1).reshape(n_row, each, LANES)
     bias = jnp.pad(bias_local[:1][None], ((0, n_row - 1), (0, 0), (0, 0)))
-    small = jnp.concatenate([small, bias], axis=1).astype(BF)
-    total = total + jnp.pad(small, ((0, 0), (main, pack - main - each - 1), (0, 0)))
+    rest = jnp.zeros((n_row, pack - main - each - 1, out), F32)
+    small = jnp.concatenate([small, bias, rest], axis=1).astype(BF)
+    total = jnp.concatenate([total.reshape(n_row, main, out), small], axis=1)
     total = scatter_blocks(total.reshape(n_row * pack, out), "row").astype(BF)
     alignment_gradient = jnp.einsum(
         "awr,iw->air", left_sum, first_projection.astype(F32), precision=exact
     ) + jnp.einsum("awr,iw->air", right_back, second_projection.astype(F32), precision=exact)
     total = jnp.sum(gather_blocks(total, "col").astype(F32), axis=0).astype(BF)
-    total = gather_blocks(total, "row")
+    total = gather_blocks(total, "row").astype(F32)
     total, left_weight, right_weight, bias = unpack(
         total, width, left_weight.shape[1], 1.0 / (owned * n_row * n_col)
     )

time: 149 us -> 149 us (level)
  Pallas kernels: 51 us -> 48.8 us
  transfers between devices with their start and end apart: 7 -> 7, of which waited for: 5 -> 5; matrix products, arithmetic and copies ran while one was open for 1% -> 1% of each run, Pallas kernels for 33% -> 31%
where the time goes in v3:
time: 149 us; the launch traced here: 148 us
  Pallas kernels  48.8 us (33%)
  starting transfers between devices  48.1 us (32%)
  blocking collectives  31.8 us (21%)
  waiting for transfers between devices  12.7 us (9%)
  local copies, waits for them, and re-layouts  2.79 us (2%)
  matrix products  1.63 us (1%)
  other arithmetic  1.49 us (1%)
    all_to_all x5, starting transfers between devices, exchange(): return lax.all_to_all(x, axis, 0, 0, tiled=True)  37.4 us
    all_to_all x2, blocking collectives, exchange(): return lax.all_to_all(x, axis, 0, 0, tiled=True)  31.8 us
    pallas_call x1, Pallas kernels, pairs(): pl.pallas_call(functools.partial(pair_kernel, width, group), grid=(rows /...  17.1 us
    all_to_all x5, waiting for transfers between devices, exchange(): return lax.all_to_all(x, axis, 0, 0, tiled=True)  10.7 us
    ppermute x2, starting transfers between devices, swap_axes(): lax.ppermute(x, ('row', 'col'), [(r * n + c, c * n + r) for r in range(n)...  10.7 us
    pallas_call x1, Pallas kernels, outer_grads(): pl.pallas_call(functools.partial(outer_grad_kernel, width, pieces), in_sp...  10.5 us
    pallas_call x1, Pallas kernels, left_grads(): pl.pallas_call(functools.partial(left_grad_kernel, scale, pieces), in_spe...  9.52 us
    pallas_call x1, Pallas kernels, right_grads(): pl.pallas_call(functools.partial(right_grad_kernel, pieces), in_specs=[pl...  8.83 us
  transfers between devices with their start and end apart: 7, of which 5 were waited for; matrix products, arithmetic and copies ran while one was open for 1% of the time, Pallas kernels for 31%

profile of v3, /device:TPU:1, one launch (start us, length us, event | category | flops | bytes accessed | tf_op | source)
XLA Modules:
  0.0 148.1 jit_solution(3579570533850421082)
XLA Ops:
  0.6 1.9 %project.1 = (bf16[16,5,32,128]{3,2,1,0:T(8,128)(2,1)}, bf16[5,32,128]{2,1,0:T(8,128)(2,1)}) custom-call(bf16[5,64,128]{2,1,0:T(8,128)(2,1)} %x_ref.1, bf16[32,64]{1,0:T(8,128)(2,1)} %bitcast.43, bf16[32,64]{1,0:T(8,128)(2,1)} %bitcast.44), custom_call_target="tpu_custom_call" | custom-call | flops 4194304 | bytes 1048576 | tf_op jit(solution)/shard_map/project/pallas_call | solution.py:51
  2.6 11.7 %all-to-all-start = ((bf16[16,5,32,128]{3,2,1,0:T(8,128)(2,1)}), bf16[16,5,32,128]{3,2,1,0:T(8,128)(2,1)S(1)}, u32[]{:S(2)}, u32[]{:S(2)}) async-start(bf16[16,5,32,128]{3,2,1,0:T(8,128)(2,1)} %get-tuple-element.23), calls=%async_computation | async-start | bytes 1310720 | tf_op jit(solution)/shard_map/all_to_all | solution.py:18
  14.3 5.3 %collective-permute-start = (bf16[5,32,128]{2,1,0:T(8,128)(2,1)}, bf16[5,32,128]{2,1,0:T(8,128)(2,1)S(1)}, u32[]{:S(2)}, u32[]{:S(2)}) collective-permute-start(bf16[5,32,128]{2,1,0:T(8,128)(2,1)} %get-tuple-element.24), channel_id=1, source_target_pairs={{0,0},{1,16},{2,32},{3,48},{4,64},{5,80},{6,96},{7,112},{8,128},{9... | collective-permute-start | bytes 122888 | tf_op jit(solution)/shard_map/ppermute | solution.py:33
  19.6 10.5 %outer_grads.1 = (bf16[2560,4096]{1,0:T(8,128)(2,1)}, f32[8,128]{1,0:T(8,128)}, bf16[1024,128]{1,0:T(8,128)(2,1)}) custom-call(bf16[80,80,128]{2,1,0:T(8,128)(2,1)} %t_ref.3, bf16[32,32,128]{2,1,0:T(8,128)(2,1)} %bitcast.46), custom_call_target="tpu_custom_call" | custom-call | flops 3355443200 | bytes 23068672 | tf_op jit(solution)/shard_map/outer_grads/pallas_call | solution.py:228
  30.1 2.0 %collective-permute-done = bf16[5,32,128]{2,1,0:T(8,128)(2,1)S(1)} collective-permute-done((bf16[5,32,128]{2,1,0:T(8,128)(2,1)}, bf16[5,32,128]{2,1,0:T(8,128)(2,1)S(1)}, u32[]{:S(2)}, u32[]{:S(2)}) %collective-permute-start) | collective-permute-done | bytes 40992 | tf_op jit(solution)/shard_map/ppermute | solution.py:33
  32.1 1.2 all-to-all-done
  33.3 0.0 copy-start
  33.3 1.1 broadcast_in_dim.11
  34.4 10.5 %all-to-all-start.1 = ((bf16[16,5,32,128]{3,2,1,0:T(8,128)(2,1)}), bf16[16,5,32,128]{3,2,1,0:T(8,128)(2,1)S(1)}, u32[]{:S(2)}, u32[]{:S(2)}) async-start(bf16[16,5,32,128]{3,2,1,0:T(8,128)(2,1)} %broadcast_in_dim.11), calls=%async_computation.1 | async-start | bytes 1310720 | tf_op jit(solution)/shard_map/all_to_all | solution.py:18
  44.9 0.0 copy-start.5
  44.9 8.8 %right_grads.1 = bf16[80,32,128]{2,1,0:T(8,128)(2,1)} custom-call(bf16[2560,128]{1,0:T(8,128)(2,1)S(1)} %bitcast.38, bf16[2560,4096]{1,0:T(8,128)(2,1)} %get-tuple-element.28.g_ref), custom_call_target="tpu_custom_call" | custom-call | flops 5368709120 | bytes 23068672 | tf_op jit(solution)/shard_map/right_grads/pallas_call | solution.py:285
  53.8 0.0 copy-done
  53.8 2.4 %all-to-all-done.1 = bf16[16,5,32,128]{3,2,1,0:T(8,128)(2,1)S(1)} async-done(((bf16[16,5,32,128]{3,2,1,0:T(8,128)(2,1)}), bf16[16,5,32,128]{3,2,1,0:T(8,128)(2,1)S(1)}, u32[]{:S(2)}, u32[]{:S(2)}) %all-to-all-start.1) | async-done | bytes 655392 | tf_op jit(solution)/shard_map/all_to_all | solution.py:18
  56.2 4.5 %all-to-all-start.2 = ((bf16[16,5,32,128]{3,2,1,0:T(8,128)(2,1)}), bf16[16,5,32,128]{3,2,1,0:T(8,128)(2,1)S(1)}, u32[]{:S(2)}, u32[]{:S(2)}) async-start(bf16[16,5,32,128]{3,2,1,0:T(8,128)(2,1)} %bitcast.6), calls=%async_computation.2 | async-start | bytes 1310720 | tf_op jit(solution)/shard_map/all_to_all | solution.py:18
  60.7 0.0 copy-done.5
  60.7 0.1 pad.9.clone
  60.8 9.5 %left_grads.1 = (bf16[2560,128]{1,0:T(8,128)(2,1)}, bf16[32,80,128]{2,1,0:T(8,128)(2,1)S(1)}) custom-call(bf16[80,32,128]{2,1,0:T(8,128)(2,1)S(1)} %bitcast.40, bf16[2560,4096]{1,0:T(8,128)(2,1)} %get-tuple-element.28.g_ref), custom_call_target="tpu_custom_call" | custom-call | flops 5368709120 | bytes 23068672 | tf_op jit(solution)/shard_map/left_grads/pallas_call | solution.py:257
  70.3 0.0 copy-start.1
  70.4 0.8 copy-done.1
  71.2 0.9 all-to-all-done.2
  72.0 3.6 %all-to-all-start.3 = ((bf16[16,5,32,128]{3,2,1,0:T(8,128)(2,1)}), bf16[16,5,32,128]{3,2,1,0:T(8,128)(2,1)S(1)}, u32[]{:S(2)}, u32[]{:S(2)}) async-start(bf16[16,5,32,128]{3,2,1,0:T(8,128)(2,1)} %bitcast.7), calls=%async_computation.3 | async-start | bytes 1310720 | tf_op jit(solution)/shard_map/all_to_all | solution.py:18
  75.6 0.1 convert_reduce_fusion.1
  75.7 5.4 %collective-permute-start.1 = (f32[5,32,128]{2,1,0:T(8,128)S(1)}, f32[5,32,128]{2,1,0:T(8,128)S(1)}, u32[]{:S(2)}, u32[]{:S(2)}) collective-permute-start(f32[5,32,128]{2,1,0:T(8,128)S(1)} %convert_reduce_fusion.1), channel_id=1, source_target_pairs={{0,0},{1,16},{2,32},{3,48},{4,64},{5,80},{6,96},{7,112},{8,128},{9... | collective-permute-start | bytes 245768 | tf_op jit(solution)/shard_map/ppermute | solution.py:33
  81.1 0.0 copy-start.2
  81.1 17.1 %pairs.1 = (bf16[80,80,128]{2,1,0:T(8,128)(2,1)}, bf16[1024,128]{1,0:T(8,128)(2,1)}) custom-call(bf16[2560,128]{1,0:T(8,128)(2,1)} %bitcast.39, bf16[32,80,128]{2,1,0:T(8,128)(2,1)} %copy-done.1, bf16[80,80,128]{2,1,0:T(8,128)(2,1)} %t_ref.3, bf16[1024,128]{1,0:T(8,128)(2,1)} %get-tuple-element.31.w_ref, f32[1,128]{1,0:T(1,128)} %bitcast.49), custom_call_target="tpu_custom_call" | custom-call | flops 16106127360 | bytes 6291456 | tf_op jit(solution)/shard_map/pairs/pallas_call | solution.py:313
  98.2 0.0 all-to-all-done.3
  98.2 0.1 convert_reduce_fusion
  98.3 0.0 copy-done.2
  98.3 0.2 fusion.1
  98.5 0.0 collective-permute-done.1
  98.6 0.2 fusion.2
  98.8 0.1 pad_maximum_fusion
  98.8 1.1 fusion.6
  99.9 0.0 copy-start.3
  99.9 0.0 copy-start.4
  100.0 17.3 %all_to_all.35 = bf16[16,72,128]{2,1,0:T(8,128)(2,1)S(1)} all-to-all(bf16[16,72,128]{2,1,0:T(8,128)(2,1)S(1)} %fusion.6), channel_id=1, replica_groups=mesh['row'=16,'col'=16] {'row'}, dimensions={0} | all-to-all | bytes 589824 | tf_op jit(solution)/shard_map/all_to_all | solution.py:18
  117.4 14.5 %all_to_all.36 = bf16[16,72,128]{2,1,0:T(8,128)(2,1)S(1)} all-to-all(bf16[16,72,128]{2,1,0:T(8,128)(2,1)S(1)} %broadcast_in_dim.28), channel_id=1, replica_groups=mesh['row'=16,'col'=16] {'col'}, dimensions={0} | all-to-all | bytes 589824 | tf_op jit(solution)/shard_map/all_to_all | solution.py:18
  131.9 0.8 broadcast_in_dim.29
  132.7 7.0 %all-to-all-start.6 = ((bf16[16,72,128]{2,1,0:T(8,128)(2,1)}), bf16[16,72,128]{2,1,0:T(8,128)(2,1)S(1)}, u32[]{:S(2)}, u32[]{:S(2)}) async-start(bf16[16,72,128]{2,1,0:T(8,128)(2,1)} %broadcast_in_dim.29), calls=%async_computation.6 | async-start | bytes 589824 | tf_op jit(solution)/shard_map/all_to_all | solution.py:18
  139.7 0.0 copy-done.3
  139.7 0.3 fusion.8
  139.9 0.0 copy-done.4
  139.9 0.9 fusion
  140.9 6.2 %all-to-all-done.6 = bf16[16,72,128]{2,1,0:T(8,128)(2,1)S(1)} async-done(((bf16[16,72,128]{2,1,0:T(8,128)(2,1)}), bf16[16,72,128]{2,1,0:T(8,128)(2,1)S(1)}, u32[]{:S(2)}, u32[]{:S(2)}) %all-to-all-start.6) | async-done | bytes 294944 | tf_op jit(solution)/shard_map/all_to_all | solution.py:18
  147.1 0.9 unpack.1
  (7 shorter events, 0.2 us)
Async XLA Ops:
  2.6 30.8 %all-to-all-start = ((bf16[16,5,32,128]{3,2,1,0:T(8,128)(2,1)}), bf16[16,5,32,128]{3,2,1,0:T(8,128)(2,1)S(1)}, u32[]{:S(2)}, u32[]{:S(2)}) async-start(bf16[16,5,32,128]{3,2,1,0:T(8,128)(2,1)} %get-tuple-element.23), calls=%async_computation | async-start | bytes 1310720 | tf_op jit(solution)/shard_map/all_to_all | solution.py:18
  14.3 17.8 %collective-permute-start = (bf16[5,32,128]{2,1,0:T(8,128)(2,1)}, bf16[5,32,128]{2,1,0:T(8,128)(2,1)S(1)}, u32[]{:S(2)}, u32[]{:S(2)}) collective-permute-start(bf16[5,32,128]{2,1,0:T(8,128)(2,1)} %get-tuple-element.24), channel_id=1, source_target_pairs={{0,0},{1,16},{2,32},{3,48},{4,64},{5,80},{6,96},{7,112},{8,128},{9... | collective-permute-start | bytes 122888 | tf_op jit(solution)/shard_map/ppermute | solution.py:33
  33.3 20.4 %copy-start = (bf16[16,5,32,128]{3,2,1,0:T(8,128)(2,1)}, bf16[16,5,32,128]{3,2,1,0:T(8,128)(2,1)S(1)}, u32[]{:S(2)}) copy-start(bf16[16,5,32,128]{3,2,1,0:T(8,128)(2,1)S(1)} %all-to-all-done) | copy-start | bytes 1966084
  34.4 21.8 %all-to-all-start.1 = ((bf16[16,5,32,128]{3,2,1,0:T(8,128)(2,1)}), bf16[16,5,32,128]{3,2,1,0:T(8,128)(2,1)S(1)}, u32[]{:S(2)}, u32[]{:S(2)}) async-start(bf16[16,5,32,128]{3,2,1,0:T(8,128)(2,1)} %broadcast_in_dim.11), calls=%async_computation.1 | async-start | bytes 1310720 | tf_op jit(solution)/shard_map/all_to_all | solution.py:18
  44.9 15.8 %copy-start.5 = (f32[8,128]{1,0:T(8,128)S(1)}, f32[8,128]{1,0:T(8,128)}, u32[]{:S(2)}) copy-start(f32[8,128]{1,0:T(8,128)} %get-tuple-element.26) | copy-start | bytes 12292
  56.2 15.9 %all-to-all-start.2 = ((bf16[16,5,32,128]{3,2,1,0:T(8,128)(2,1)}), bf16[16,5,32,128]{3,2,1,0:T(8,128)(2,1)S(1)}, u32[]{:S(2)}, u32[]{:S(2)}) async-start(bf16[16,5,32,128]{3,2,1,0:T(8,128)(2,1)} %bitcast.6), calls=%async_computation.2 | async-start | bytes 1310720 | tf_op jit(solution)/shard_map/all_to_all | solution.py:18
  70.3 0.8 copy-start.1
  72.0 26.2 %all-to-all-start.3 = ((bf16[16,5,32,128]{3,2,1,0:T(8,128)(2,1)}), bf16[16,5,32,128]{3,2,1,0:T(8,128)(2,1)S(1)}, u32[]{:S(2)}, u32[]{:S(2)}) async-start(bf16[16,5,32,128]{3,2,1,0:T(8,128)(2,1)} %bitcast.7), calls=%async_computation.3 | async-start | bytes 1310720 | tf_op jit(solution)/shard_map/all_to_all | solution.py:18
  75.7 22.8 %collective-permute-start.1 = (f32[5,32,128]{2,1,0:T(8,128)S(1)}, f32[5,32,128]{2,1,0:T(8,128)S(1)}, u32[]{:S(2)}, u32[]{:S(2)}) collective-permute-start(f32[5,32,128]{2,1,0:T(8,128)S(1)} %convert_reduce_fusion.1), channel_id=1, source_target_pairs={{0,0},{1,16},{2,32},{3,48},{4,64},{5,80},{6,96},{7,112},{8,128},{9... | collective-permute-start | bytes 245768 | tf_op jit(solution)/shard_map/ppermute | solution.py:33
  81.1 17.2 %copy-start.2 = (bf16[5,64,128]{2,1,0:T(8,128)(2,1)S(1)}, bf16[5,64,128]{2,1,0:T(8,128)(2,1)}, u32[]{:S(2)}) copy-start(bf16[5,64,128]{2,1,0:T(8,128)(2,1)} %x_ref.1) | copy-start | bytes 245764
  99.9 39.7 %copy-start.3 = (bf16[64,32]{0,1:T(8,128)(2,1)S(1)}, bf16[64,32]{0,1:T(8,128)(2,1)}, u32[]{:S(2)}) copy-start(bf16[64,32]{0,1:T(8,128)(2,1)} %param.7) | copy-start | bytes 12292
  99.9 40.0 %copy-start.4 = (bf16[64,32]{0,1:T(8,128)(2,1)S(1)}, bf16[64,32]{0,1:T(8,128)(2,1)}, u32[]{:S(2)}) copy-start(bf16[64,32]{0,1:T(8,128)(2,1)} %param.8) | copy-start | bytes 12292
  132.7 14.4 %all-to-all-start.6 = ((bf16[16,72,128]{2,1,0:T(8,128)(2,1)}), bf16[16,72,128]{2,1,0:T(8,128)(2,1)S(1)}, u32[]{:S(2)}, u32[]{:S(2)}) async-start(bf16[16,72,128]{2,1,0:T(8,128)(2,1)} %broadcast_in_dim.29), calls=%async_computation.6 | async-start | bytes 589824 | tf_op jit(solution)/shard_map/all_to_all | solution.py:18
